TPU v7x, 32 devices: a whole 2x2x4 slice. The times are simulated.
32 devices in a mesh: dp: 4 (over z), seq: 8 (over y, x, core).
Axes of the slice: x: 2, y: 2, z: 4, core: 2. Of those that a mesh axis runs over, the one named last changes fastest.
Arguments:
- enc_input: bfloat16 [8, 512, 768], P('dp', 'seq'), may hold values from -6 to 6
- dec_input: bfloat16 [8, 512, 768], P('dp', 'seq'), may hold values from -6 to 6
- enc_lengths: int32 [8], P('dp'), may hold values from 128 to 512, as said below
- dec_lengths: int32 [8], P('dp'), may hold values from 128 to 512, as said below
- enc_buckets: int32 [1023], replicated, may hold values from 0 to 31
- dec_buckets: int32 [512], replicated, may hold values from 0 to 31
- attention_in: bfloat16 [3, 3, 768, 768], P(None, None, ('dp', 'seq')), may hold values from -0.21875 to 0.21875
- attention_out: bfloat16 [3, 768, 768], P(None, ('dp', 'seq')), may hold values from -0.875 to 0.875
- hidden_in: bfloat16 [2, 2, 768, 2048], P(None, None, ('dp', 'seq')), may hold values from -0.21875 to 0.21875
- hidden_out: bfloat16 [2, 2048, 768], P(None, ('dp', 'seq')), may hold values from -0.25 to 0.25
- norm_gains: bfloat16 [7, 768], P(None, ('dp', 'seq')), may hold values from 0.5 to 1.5
- position_bias: float32 [2, 32, 12], replicated, may hold values from -4 to 4
- enc_cotangent: bfloat16 [8, 512, 768], P('dp', 'seq'), may hold values from -6 to 6
- dec_cotangent: bfloat16 [8, 512, 768], P('dp', 'seq'), may hold values from -6 to 6
Outputs:
- enc_output: bfloat16 [8, 512, 768], P('dp', 'seq')
- dec_output: bfloat16 [8, 512, 768], P('dp', 'seq')
- grad_enc_input: float32 [8, 512, 768], P('dp', 'seq')
- grad_dec_input: float32 [8, 512, 768], P('dp', 'seq')
- grad_attention_in: float32 [3, 3, 768, 768], P(None, None, ('dp', 'seq'))
- grad_attention_out: float32 [3, 768, 768], P(None, ('dp', 'seq'))
- grad_hidden_in: float32 [2, 2, 768, 2048], P(None, None, ('dp', 'seq'))
- grad_hidden_out: float32 [2, 2048, 768], P(None, ('dp', 'seq'))
- grad_norm_gains: float32 [7, 768], P(None, ('dp', 'seq'))
- grad_position_bias: float32 [2, 32, 12], replicated
- row_attention_in: float32 [3, 3, 768], P(None, None, ('dp', 'seq'))
- col_attention_in: float32 [3, 3, 768], replicated
- row_attention_out: float32 [3, 768], P(None, ('dp', 'seq'))
- col_attention_out: float32 [3, 768], replicated
- row_hidden_in: float32 [2, 2, 768], P(None, None, ('dp', 'seq'))
- col_hidden_in: float32 [2, 2, 2048], replicated
- row_hidden_out: float32 [2, 2048], P(None, ('dp', 'seq'))
- col_hidden_out: float32 [2, 768], replicated
Inputs may be any that keep to these rules, and one draw needn't show every extreme that they name: `enc_lengths`: among the 2 sequences of one dp index at least one has all 512 valid tokens. `dec_lengths`: among the 2 sequences of one dp index at least one has all 512 valid tokens.
All inputs are finite; a program needn't handle non-finite values.
Results may differ from a plain program's by a relative error of at most 0.04.
Values may be sent and summed in bfloat16 or wider, within the bound.
No kernel may reach another device: no remote copies, remote signals or barrier semaphores. Data moves between devices by JAX's collectives and lax.ppermute only.
A program may use at most 384 MiB of HBM per device.

v0:
```python
import math

import jax
import jax.numpy as jnp
from jax import lax
from jax.sharding import PartitionSpec as P

D = 768
HEADS = 12
HEAD = 64
FF = 2048


EPSILON = 1e-06
NEGATIVE = -1e30
HIGHEST = lax.Precision.HIGHEST


def rounded(values):
    return values.astype(jnp.bfloat16)


def rows_first(values):
    return values.transpose(0, 2, 1)


def rms_norm(values, gain_row):
    return (
        values * lax.rsqrt(jnp.mean(values * values, axis=-1, keepdims=True) + EPSILON) * gain_row
    )


def rms_back(values, gain_row, upstream):
    _, pullback = jax.vjp(rms_norm, values, gain_row)
    return pullback(upstream)


def gated_unit(gate_up):
    return jax.nn.gelu(gate_up[0], approximate=True) * gate_up[1]


def offset_table(buckets, layer_bias):
    choose = (buckets[:, None] == jnp.arange(layer_bias.shape[0], dtype=jnp.int32)[None, :]).astype(
        jnp.float32
    )
    return jnp.dot(choose, layer_bias, precision=HIGHEST).T


def bucket_grad(buckets, grad_bias, bucket_count):
    choose = (buckets[:, None] == jnp.arange(bucket_count, dtype=jnp.int32)[None, :]).astype(
        jnp.float32
    )
    return jnp.dot(choose.T, grad_bias.T, precision=HIGHEST)


def hankel_block(window, rows, cols):
    heads_here, length = (window.shape[0], window.shape[1])
    tiled = jnp.tile(window, (1, rows + 1))[:, : rows * (length + 1)]
    return tiled.reshape(heads_here, rows, length + 1)[:, :, :cols]


def bias_block(variant, table, row_start, col_start, rows, cols, extent):
    span = rows + cols - 1
    if variant == "enc":
        base = col_start - row_start - (rows - 1) + (extent - 1)
        window = lax.dynamic_slice_in_dim(table, base, span, 1)
        return hankel_block(window, rows, cols)[:, ::-1, :]
    widened = jnp.concatenate(
        [jnp.broadcast_to(table[:, :1], (table.shape[0], extent - 1)), table], axis=1
    )
    base = row_start - col_start - (cols - 1) + (extent - 1)
    window = lax.dynamic_slice_in_dim(widened, base, span, 1)
    return hankel_block(window, rows, cols)[:, :, ::-1]


def visible_mask(variant, row_ids, col_ids, lengths):
    visible = col_ids[None, None, :] < lengths[:, None, None]
    if variant == "dec":
        visible = visible & (col_ids[None, None, :] <= row_ids[None, :, None])
    return visible[:, None]


def block_scores(query_heads, key_heads, row_ids, col_ids, lengths, variant, offset_bias, extent):
    factor = HEAD ** (-0.5)
    scores = (
        jnp.einsum("sqhe,skhe->shqk", query_heads, key_heads, preferred_element_type=jnp.float32)
        * factor
    )
    if offset_bias is not None:
        scores = (
            scores
            + bias_block(
                variant,
                offset_bias,
                row_ids[0],
                col_ids[0],
                row_ids.shape[0],
                col_ids.shape[0],
                extent,
            )[None]
        )
    return (scores, visible_mask(variant, row_ids, col_ids, lengths))


def row_products(grad_context, context):
    seqs_here, rows_here = (context.shape[0], context.shape[1])
    return jnp.sum(
        (grad_context.astype(jnp.float32) * context).reshape(seqs_here, rows_here, HEADS, HEAD),
        axis=-1,
    ).transpose(0, 2, 1)


def attend(queries, row_ids, lengths, variant, offset_bias, extent, fold_keys):
    seqs_here, rows_here = (queries.shape[0], queries.shape[1])
    query_heads = queries.reshape(seqs_here, rows_here, HEADS, HEAD)

    def fold_step(carried, pieces, begin_at):
        key_rows, value_rows = pieces
        block_len = math.gcd(key_rows.shape[1], 512)

        def block_step(block_id, running):
            row_max, row_sum, weighted = running
            offset_in = block_id * block_len
            key_heads = lax.dynamic_slice_in_dim(key_rows, offset_in, block_len, 1).reshape(
                seqs_here, block_len, HEADS, HEAD
            )
            value_heads = lax.dynamic_slice_in_dim(value_rows, offset_in, block_len, 1).reshape(
                seqs_here, block_len, HEADS, HEAD
            )
            col_ids = offset_in + jnp.arange(block_len, dtype=jnp.int32)
            scores, visible = block_scores(
                query_heads, key_heads, row_ids, col_ids, lengths, variant, offset_bias, extent
            )
            new_max = jnp.maximum(row_max, jnp.max(jnp.where(visible, scores, NEGATIVE), axis=-1))
            weights = jnp.where(visible, jnp.exp(scores - new_max[..., None]), 0.0)
            shrink = jnp.exp(row_max - new_max)
            row_sum = row_sum * shrink + jnp.sum(weights, axis=-1)
            weighted = weighted * shrink[..., None] + jnp.einsum(
                "shqk,skhe->shqe", rounded(weights), value_heads, preferred_element_type=jnp.float32
            )
            return (new_max, row_sum, weighted)

        return lax.fori_loop(0, key_rows.shape[1] // block_len, block_step, carried)

    initial = (
        jnp.full((seqs_here, HEADS, rows_here), NEGATIVE, jnp.float32),
        jnp.zeros((seqs_here, HEADS, rows_here), jnp.float32),
        jnp.zeros((seqs_here, HEADS, rows_here, HEAD), jnp.float32),
    )
    row_max, row_sum, weighted = fold_keys(fold_step, initial)
    context = (
        (weighted / row_sum[..., None])
        .transpose(0, 2, 1, 3)
        .reshape(seqs_here, rows_here, HEADS * HEAD)
    )
    return (context, row_max + jnp.log(row_sum))


def attend_back(
    queries,
    log_sums,
    row_dots,
    grad_context,
    row_ids,
    lengths,
    variant,
    offset_bias,
    extent,
    fold_keys,
):
    seqs_here, rows_here = (queries.shape[0], queries.shape[1])
    query_heads = queries.reshape(seqs_here, rows_here, HEADS, HEAD)
    grad_heads = grad_context.reshape(seqs_here, rows_here, HEADS, HEAD)
    bias_width = offset_bias.shape[1] if offset_bias is not None else 1
    factor = HEAD ** (-0.5)

    def fold_step(carried, pieces, begin_at):
        key_rows, value_rows = pieces
        block_len = math.gcd(key_rows.shape[1], 512)

        def block_step(block_id, running):
            grad_query, grad_bias = (running[0], running[-1])
            offset_in = block_id * block_len
            key_heads = lax.dynamic_slice_in_dim(key_rows, offset_in, block_len, 1).reshape(
                seqs_here, block_len, HEADS, HEAD
            )
            value_heads = lax.dynamic_slice_in_dim(value_rows, offset_in, block_len, 1).reshape(
                seqs_here, block_len, HEADS, HEAD
            )
            col_ids = offset_in + jnp.arange(block_len, dtype=jnp.int32)
            scores, visible = block_scores(
                query_heads, key_heads, row_ids, col_ids, lengths, variant, offset_bias, extent
            )
            weights = jnp.where(visible, jnp.exp(scores - log_sums[..., None]), 0.0)
            grad_weights = jnp.einsum(
                "sqhe,skhe->shqk", grad_heads, value_heads, preferred_element_type=jnp.float32
            )
            grad_scores = weights * (grad_weights - row_dots[..., None])
            if offset_bias is not None:

                def table_block(table_values):
                    return bias_block(
                        variant,
                        table_values,
                        row_ids[0],
                        col_ids[0],
                        row_ids.shape[0],
                        col_ids.shape[0],
                        extent,
                    )

                _, table_pull = jax.vjp(table_block, offset_bias)
                grad_bias = grad_bias + table_pull(jnp.sum(grad_scores, axis=0))[0]
            grad_raw = rounded(grad_scores * factor)
            grad_query = grad_query + jnp.einsum(
                "shqk,skhe->shqe", grad_raw, key_heads, preferred_element_type=jnp.float32
            )
            return (grad_query, grad_bias)

        return lax.fori_loop(0, key_rows.shape[1] // block_len, block_step, carried)

    query_start = jnp.zeros((seqs_here, HEADS, rows_here, HEAD), jnp.float32)
    bias_start = jnp.zeros((HEADS, bias_width), jnp.float32)
    initial = (query_start, bias_start)
    result = fold_keys(fold_step, initial)
    grad_query = result[0].transpose(0, 2, 1, 3).reshape(seqs_here, rows_here, HEADS * HEAD)
    return (grad_query, None, None, result[1])


def owned_key_grads(
    key_rows, value_rows, col_ids, lengths, variant, offset_bias, extent, fold_queries
):
    seqs_here, keys_here = (key_rows.shape[0], key_rows.shape[1])
    key_heads = key_rows.reshape(seqs_here, keys_here, HEADS, HEAD)
    value_heads = value_rows.reshape(seqs_here, keys_here, HEADS, HEAD)
    factor = HEAD ** (-0.5)

    def fold_step(carried, pieces, begin_at):
        query_rows, grad_rows, log_rows, dot_rows = pieces
        block_len = math.gcd(query_rows.shape[1], 512)

        def block_step(block_id, running):
            grad_keys, grad_values = running
            offset_in = block_id * block_len
            query_heads = lax.dynamic_slice_in_dim(query_rows, offset_in, block_len, 1).reshape(
                seqs_here, block_len, HEADS, HEAD
            )
            grad_heads = lax.dynamic_slice_in_dim(grad_rows, offset_in, block_len, 1).reshape(
                seqs_here, block_len, HEADS, HEAD
            )
            log_block = lax.dynamic_slice_in_dim(log_rows, offset_in, block_len, 1).transpose(
                0, 2, 1
            )
            dot_block = lax.dynamic_slice_in_dim(dot_rows, offset_in, block_len, 1).transpose(
                0, 2, 1
            )
            row_ids = offset_in + jnp.arange(block_len, dtype=jnp.int32)
            scores, visible = block_scores(
                query_heads, key_heads, row_ids, col_ids, lengths, variant, offset_bias, extent
            )
            weights = jnp.where(visible, jnp.exp(scores - log_block[..., None]), 0.0)
            grad_weights = jnp.einsum(
                "sqhe,skhe->shqk", grad_heads, value_heads, preferred_element_type=jnp.float32
            )
            grad_scores = weights * (grad_weights - dot_block[..., None])
            grad_raw = rounded(grad_scores * factor)
            grad_keys = grad_keys + jnp.einsum(
                "shqk,sqhe->skhe", grad_raw, query_heads, preferred_element_type=jnp.float32
            ).reshape(seqs_here, keys_here, HEADS * HEAD)
            grad_values = grad_values + jnp.einsum(
                "shqk,sqhe->skhe", rounded(weights), grad_heads, preferred_element_type=jnp.float32
            ).reshape(seqs_here, keys_here, HEADS * HEAD)
            return (grad_keys, grad_values)

        return lax.fori_loop(0, query_rows.shape[1] // block_len, block_step, carried)

    initial = (
        jnp.zeros((seqs_here, keys_here, HEADS * HEAD), jnp.float32),
        jnp.zeros((seqs_here, keys_here, HEADS * HEAD), jnp.float32),
    )
    return fold_queries(fold_step, initial)


def feed_forward(residual, gain_row, weights_in, weights_out):
    normed_low = rounded(rms_norm(residual, gain_row))
    gate_up = jnp.einsum(
        "srd,jdf->jsrf", normed_low, weights_in, preferred_element_type=jnp.float32
    )
    hidden = rounded(gated_unit(gate_up))
    output = jnp.einsum("srf,fd->srd", hidden, weights_out, preferred_element_type=jnp.float32)
    return (residual + output, (normed_low, gate_up, hidden))


def feed_back(residual, gain_row, weights_in, weights_out, kept_values, upstream):
    normed_low, gate_up, hidden = kept_values
    upstream_low = rounded(upstream)
    grad_out_weights = jnp.einsum(
        "srf,srd->fd", hidden, upstream_low, preferred_element_type=jnp.float32
    )
    grad_hidden = jnp.einsum(
        "srd,fd->srf", upstream_low, weights_out, preferred_element_type=jnp.float32
    )
    _, pullback = jax.vjp(gated_unit, gate_up)
    grad_gate_up = rounded(pullback(grad_hidden)[0])
    grad_in_weights = jnp.einsum(
        "srd,jsrf->jdf", normed_low, grad_gate_up, preferred_element_type=jnp.float32
    )
    grad_normed = jnp.einsum(
        "jsrf,jdf->srd", grad_gate_up, weights_in, preferred_element_type=jnp.float32
    )
    grad_residual, grad_gain = rms_back(residual, gain_row, grad_normed)
    return (upstream + grad_residual, grad_gain, grad_in_weights, grad_out_weights)


def local(
    enc_input,
    dec_input,
    enc_lengths,
    dec_lengths,
    enc_buckets,
    dec_buckets,
    attention_in,
    attention_out,
    hidden_in,
    hidden_out,
    norm_gains,
    position_bias,
    enc_cotangent,
    dec_cotangent,
):
    full_in, full_out, full_hidden_in, full_hidden_out, full_gains = (
        lax.all_gather(attention_in, ("dp", "seq"), axis=2, tiled=True),
        lax.all_gather(attention_out, ("dp", "seq"), axis=1, tiled=True),
        lax.all_gather(hidden_in, ("dp", "seq"), axis=2, tiled=True),
        lax.all_gather(hidden_out, ("dp", "seq"), axis=1, tiled=True),
        lax.all_gather(norm_gains, ("dp", "seq"), axis=1, tiled=True),
    )
    gain_rows = full_gains.astype(jnp.float32)
    enc_rows = enc_input.shape[1]
    dec_rows = dec_input.shape[1]
    seq_index = lax.axis_index("seq")
    enc_ids = seq_index * enc_rows + jnp.arange(enc_rows, dtype=jnp.int32)
    dec_ids = seq_index * dec_rows + jnp.arange(dec_rows, dtype=jnp.int32)
    enc_extent = (enc_buckets.shape[0] + 1) // 2
    dec_extent = dec_buckets.shape[0]
    enc_table = offset_table(enc_buckets, position_bias[0])
    dec_table = offset_table(dec_buckets, position_bias[1])
    enc_values = enc_input.astype(jnp.float32)
    norm_a_low = rounded(rms_norm(enc_values, gain_rows[0]))
    enc_qkv = rounded(
        jnp.einsum("srd,jde->jsre", norm_a_low, full_in[0], preferred_element_type=jnp.float32)
    )
    enc_context, enc_logs = attend(
        enc_qkv[0],
        enc_ids,
        enc_lengths,
        "enc",
        enc_table,
        enc_extent,
        lambda folder, initial: folder(
            initial,
            (
                lax.all_gather(enc_qkv[1], "seq", axis=1, tiled=True),
                lax.all_gather(enc_qkv[2], "seq", axis=1, tiled=True),
            ),
            jnp.int32(0),
        ),
    )
    enc_context_low = rounded(enc_context)
    enc_mid = enc_values + jnp.einsum(
        "srd,de->sre", enc_context_low, full_out[0], preferred_element_type=jnp.float32
    )
    enc_last, enc_ffn_kept = feed_forward(
        enc_mid, gain_rows[1], full_hidden_in[0], full_hidden_out[0]
    )
    memory = rms_norm(enc_last, gain_rows[2])
    memory_low = rounded(memory)
    dec_values = dec_input.astype(jnp.float32)
    norm_b_low = rounded(rms_norm(dec_values, gain_rows[3]))
    dec_qkv = rounded(
        jnp.einsum("srd,jde->jsre", norm_b_low, full_in[1], preferred_element_type=jnp.float32)
    )
    dec_context, dec_logs = attend(
        dec_qkv[0],
        dec_ids,
        dec_lengths,
        "dec",
        dec_table,
        dec_extent,
        lambda folder, initial: folder(
            initial,
            (
                lax.all_gather(dec_qkv[1], "seq", axis=1, tiled=True),
                lax.all_gather(dec_qkv[2], "seq", axis=1, tiled=True),
            ),
            jnp.int32(0),
        ),
    )
    dec_context_low = rounded(dec_context)
    dec_mid = dec_values + jnp.einsum(
        "srd,de->sre", dec_context_low, full_out[1], preferred_element_type=jnp.float32
    )
    norm_c_low = rounded(rms_norm(dec_mid, gain_rows[4]))
    cross_query = rounded(
        jnp.einsum("srd,de->sre", norm_c_low, full_in[2, 0], preferred_element_type=jnp.float32)
    )
    cross_pair = rounded(
        jnp.einsum("srd,jde->jsre", memory_low, full_in[2, 1:], preferred_element_type=jnp.float32)
    )
    cross_context, cross_logs = attend(
        cross_query,
        dec_ids,
        enc_lengths,
        "cross",
        None,
        0,
        lambda folder, initial: folder(
            initial,
            (
                lax.all_gather(cross_pair[0], "seq", axis=1, tiled=True),
                lax.all_gather(cross_pair[1], "seq", axis=1, tiled=True),
            ),
            jnp.int32(0),
        ),
    )
    cross_low = rounded(cross_context)
    dec_cross = dec_mid + jnp.einsum(
        "srd,de->sre", cross_low, full_out[2], preferred_element_type=jnp.float32
    )
    dec_last, dec_ffn_kept = feed_forward(
        dec_cross, gain_rows[5], full_hidden_in[1], full_hidden_out[1]
    )
    dec_final = rms_norm(dec_last, gain_rows[6])
    grad_dec_last, grad_gain_six = rms_back(
        dec_last, gain_rows[6], dec_cotangent.astype(jnp.float32)
    )
    grad_dec_cross, grad_gain_five, grad_hin_one, grad_hout_one = feed_back(
        dec_cross, gain_rows[5], full_hidden_in[1], full_hidden_out[1], dec_ffn_kept, grad_dec_last
    )
    upstream_low = rounded(grad_dec_cross)
    grad_out_two = jnp.einsum(
        "srd,sre->de", cross_low, upstream_low, preferred_element_type=jnp.float32
    )
    grad_cross_context = rounded(
        jnp.einsum("sre,de->srd", upstream_low, full_out[2], preferred_element_type=jnp.float32)
    )
    cross_dots = row_products(grad_cross_context, cross_context)
    cross_grad_query, cross_grad_keys, cross_grad_values, _ = attend_back(
        cross_query,
        cross_logs,
        cross_dots,
        grad_cross_context,
        dec_ids,
        enc_lengths,
        "cross",
        None,
        0,
        lambda folder, initial: folder(
            initial,
            (
                lax.all_gather(cross_pair[0], "seq", axis=1, tiled=True),
                lax.all_gather(cross_pair[1], "seq", axis=1, tiled=True),
            ),
            jnp.int32(0),
        ),
    )
    cross_query_low = rounded(cross_grad_query)
    grad_query_two = jnp.einsum(
        "srd,sre->de", norm_c_low, cross_query_low, preferred_element_type=jnp.float32
    )
    grad_norm_c = jnp.einsum(
        "sre,de->srd", cross_query_low, full_in[2, 0], preferred_element_type=jnp.float32
    )
    grad_mid_part, grad_gain_four = rms_back(dec_mid, gain_rows[4], grad_norm_c)
    grad_dec_mid = grad_dec_cross + grad_mid_part
    upstream_low = rounded(grad_dec_mid)
    grad_out_one = jnp.einsum(
        "srd,sre->de", dec_context_low, upstream_low, preferred_element_type=jnp.float32
    )
    grad_dec_context = rounded(
        jnp.einsum("sre,de->srd", upstream_low, full_out[1], preferred_element_type=jnp.float32)
    )
    dec_dots = row_products(grad_dec_context, dec_context)
    dec_grad_query, dec_grad_keys, dec_grad_values, grad_dec_bias = attend_back(
        dec_qkv[0],
        dec_logs,
        dec_dots,
        grad_dec_context,
        dec_ids,
        dec_lengths,
        "dec",
        dec_table,
        dec_extent,
        lambda folder, initial: folder(
            initial,
            (
                lax.all_gather(dec_qkv[1], "seq", axis=1, tiled=True),
                lax.all_gather(dec_qkv[2], "seq", axis=1, tiled=True),
            ),
            jnp.int32(0),
        ),
    )
    cross_key_grad, cross_value_grad = owned_key_grads(
        cross_pair[0],
        cross_pair[1],
        enc_ids,
        enc_lengths,
        "cross",
        None,
        0,
        lambda folder, initial: folder(
            initial,
            (
                lax.all_gather(cross_query, "seq", axis=1, tiled=True),
                lax.all_gather(grad_cross_context, "seq", axis=1, tiled=True),
                lax.all_gather(
                    rows_first(cross_logs).astype(jnp.bfloat16), "seq", axis=1, tiled=True
                ).astype(jnp.float32),
                lax.all_gather(
                    rows_first(cross_dots).astype(jnp.bfloat16), "seq", axis=1, tiled=True
                ).astype(jnp.float32),
            ),
            jnp.int32(0),
        ),
    )
    dec_key_grad, dec_value_grad = owned_key_grads(
        dec_qkv[1],
        dec_qkv[2],
        dec_ids,
        dec_lengths,
        "dec",
        dec_table,
        dec_extent,
        lambda folder, initial: folder(
            initial,
            (
                lax.all_gather(dec_qkv[0], "seq", axis=1, tiled=True),
                lax.all_gather(grad_dec_context, "seq", axis=1, tiled=True),
                lax.all_gather(
                    rows_first(dec_logs).astype(jnp.bfloat16), "seq", axis=1, tiled=True
                ).astype(jnp.float32),
                lax.all_gather(
                    rows_first(dec_dots).astype(jnp.bfloat16), "seq", axis=1, tiled=True
                ).astype(jnp.float32),
            ),
            jnp.int32(0),
        ),
    )
    pair_grads = rounded(jnp.stack([cross_key_grad, cross_value_grad]))
    grad_pair_two = jnp.einsum(
        "srd,jsre->jde", memory_low, pair_grads, preferred_element_type=jnp.float32
    )
    grad_memory = jnp.einsum(
        "jsre,jde->srd", pair_grads, full_in[2, 1:], preferred_element_type=jnp.float32
    )
    dec_grads = rounded(jnp.stack([dec_grad_query, dec_key_grad, dec_value_grad]))
    grad_in_one = jnp.einsum(
        "srd,jsre->jde", norm_b_low, dec_grads, preferred_element_type=jnp.float32
    )
    grad_norm_b = jnp.einsum(
        "jsre,jde->srd", dec_grads, full_in[1], preferred_element_type=jnp.float32
    )
    grad_dec_part, grad_gain_three = rms_back(dec_values, gain_rows[3], grad_norm_b)
    grad_dec_input = grad_dec_mid + grad_dec_part
    grad_memory_total = enc_cotangent.astype(jnp.float32) + grad_memory
    grad_enc_last, grad_gain_two = rms_back(enc_last, gain_rows[2], grad_memory_total)
    grad_enc_mid, grad_gain_one, grad_hin_zero, grad_hout_zero = feed_back(
        enc_mid, gain_rows[1], full_hidden_in[0], full_hidden_out[0], enc_ffn_kept, grad_enc_last
    )
    upstream_low = rounded(grad_enc_mid)
    grad_out_zero = jnp.einsum(
        "srd,sre->de", enc_context_low, upstream_low, preferred_element_type=jnp.float32
    )
    grad_enc_context = rounded(
        jnp.einsum("sre,de->srd", upstream_low, full_out[0], preferred_element_type=jnp.float32)
    )
    enc_dots = row_products(grad_enc_context, enc_context)
    enc_grad_query, enc_grad_keys, enc_grad_values, grad_enc_bias = attend_back(
        enc_qkv[0],
        enc_logs,
        enc_dots,
        grad_enc_context,
        enc_ids,
        enc_lengths,
        "enc",
        enc_table,
        enc_extent,
        lambda folder, initial: folder(
            initial,
            (
                lax.all_gather(enc_qkv[1], "seq", axis=1, tiled=True),
                lax.all_gather(enc_qkv[2], "seq", axis=1, tiled=True),
            ),
            jnp.int32(0),
        ),
    )
    enc_key_grad, enc_value_grad = owned_key_grads(
        enc_qkv[1],
        enc_qkv[2],
        enc_ids,
        enc_lengths,
        "enc",
        enc_table,
        enc_extent,
        lambda folder, initial: folder(
            initial,
            (
                lax.all_gather(enc_qkv[0], "seq", axis=1, tiled=True),
                lax.all_gather(grad_enc_context, "seq", axis=1, tiled=True),
                lax.all_gather(
                    rows_first(enc_logs).astype(jnp.bfloat16), "seq", axis=1, tiled=True
                ).astype(jnp.float32),
                lax.all_gather(
                    rows_first(enc_dots).astype(jnp.bfloat16), "seq", axis=1, tiled=True
                ).astype(jnp.float32),
            ),
            jnp.int32(0),
        ),
    )
    enc_grads = rounded(jnp.stack([enc_grad_query, enc_key_grad, enc_value_grad]))
    grad_in_zero = jnp.einsum(
        "srd,jsre->jde", norm_a_low, enc_grads, preferred_element_type=jnp.float32
    )
    grad_norm_a = jnp.einsum(
        "jsre,jde->srd", enc_grads, full_in[0], preferred_element_type=jnp.float32
    )
    grad_enc_part, grad_gain_zero = rms_back(enc_values, gain_rows[0], grad_norm_a)
    grad_enc_input = grad_enc_mid + grad_enc_part
    grad_cross_in = jnp.concatenate([grad_query_two[None], grad_pair_two], axis=0)
    grad_attention_in = jnp.stack([grad_in_zero, grad_in_one, grad_cross_in])
    grad_attention_out = jnp.stack([grad_out_zero, grad_out_one, grad_out_two])
    grad_hidden_in = jnp.stack([grad_hin_zero, grad_hin_one])
    grad_hidden_out = jnp.stack([grad_hout_zero, grad_hout_one])
    grad_gains = jnp.stack(
        [
            grad_gain_zero,
            grad_gain_one,
            grad_gain_two,
            grad_gain_three,
            grad_gain_four,
            grad_gain_five,
            grad_gain_six,
        ]
    )
    shard_in, shard_out, shard_hin, shard_hout, shard_gains = (
        lax.psum_scatter(grad_attention_in, ("dp", "seq"), scatter_dimension=2, tiled=True),
        lax.psum_scatter(grad_attention_out, ("dp", "seq"), scatter_dimension=1, tiled=True),
        lax.psum_scatter(grad_hidden_in, ("dp", "seq"), scatter_dimension=2, tiled=True),
        lax.psum_scatter(grad_hidden_out, ("dp", "seq"), scatter_dimension=1, tiled=True),
        lax.psum_scatter(grad_gains, ("dp", "seq"), scatter_dimension=1, tiled=True),
    )
    bucket_count = position_bias.shape[1]
    grad_position = jnp.stack(
        [
            bucket_grad(enc_buckets, grad_enc_bias, bucket_count),
            bucket_grad(dec_buckets, grad_dec_bias, bucket_count),
        ]
    )
    squares_in = shard_in * shard_in
    squares_out = shard_out * shard_out
    squares_hin = shard_hin * shard_hin
    squares_hout = shard_hout * shard_hout
    col_in, col_out, col_hin, col_hout, grad_position = lax.psum(
        (
            jnp.sum(squares_in, axis=2),
            jnp.sum(squares_out, axis=1),
            jnp.sum(squares_hin, axis=2),
            jnp.sum(squares_hout, axis=1),
            grad_position,
        ),
        ("dp", "seq"),
    )
    return (
        rounded(memory),
        rounded(dec_final),
        grad_enc_input,
        grad_dec_input,
        shard_in,
        shard_out,
        shard_hin,
        shard_hout,
        shard_gains,
        grad_position,
        0.5 * jnp.mean(squares_in, axis=-1),
        0.5 * col_in / D,
        0.5 * jnp.mean(squares_out, axis=-1),
        0.5 * col_out / D,
        0.5 * jnp.mean(squares_hin, axis=-1),
        0.5 * col_hin / D,
        0.5 * jnp.mean(squares_hout, axis=-1),
        0.5 * col_hout / FF,
    )


def solution(mesh):
    return jax.shard_map(
        local,
        mesh=mesh,
        in_specs=(
            P("dp", "seq", None),
            P("dp", "seq", None),
            P("dp"),
            P("dp"),
            P(),
            P(),
            P(None, None, ("dp", "seq"), None),
            P(None, ("dp", "seq"), None),
            P(None, None, ("dp", "seq"), None),
            P(None, ("dp", "seq"), None),
            P(None, ("dp", "seq")),
            P(),
            P("dp", "seq", None),
            P("dp", "seq", None),
        ),
        out_specs=(
            P("dp", "seq", None),
            P("dp", "seq", None),
            P("dp", "seq", None),
            P("dp", "seq", None),
            P(None, None, ("dp", "seq"), None),
            P(None, ("dp", "seq"), None),
            P(None, None, ("dp", "seq"), None),
            P(None, ("dp", "seq"), None),
            P(None, ("dp", "seq")),
            P(),
            P(None, None, ("dp", "seq")),
            P(),
            P(None, ("dp", "seq")),
            P(),
            P(None, None, ("dp", "seq")),
            P(),
            P(None, ("dp", "seq")),
            P(),
        ),
        check_vma=False,
    )
```

profile of v0, /device:TPU:0, one launch (start us, length us, event | category | flops | bytes accessed | tf_op | source)
XLA Modules:
  0.0 1937.5 jit_solution(17888165133756003665)
XLA Ops:
  8.0 43.9 %all-gather.8 = bf16[32,24,7]{1,2,0:T(8,128)(2,1)S(1)} all-gather(bf16[1,24,7]{1,2,0:T(8,128)(2,1)} %bitcast.576), channel_id=1, replica_groups=mesh['dp'=4,'seq'=8] {'dp','seq'}, dimensions={0}, use_global_device_ids=true | all-gather | bytes 11088 | tf_op jit(solution)/shard_map/all_gather | solution.py:336
  54.0 47.0 %all-gather.26.cloned.1.call-done = bf16[3,3,768,768]{3,2,1,0:T(8,128)(2,1)} async-done(((bf16[3,3,24,768]{3,2,1,0:T(8,128)(2,1)}), bf16[3,3,768,768]{3,2,1,0:T(8,128)(2,1)}) %all-gather.26.cloned.1.call-update) | async-done | bytes 10616848 | tf_op jit(solution)/shard_map/all_gather | solution.py:332
  136.7 19.9 %all-gather.44.cloned.1.call-done = bf16[1,2,512,768]{3,2,0,1:T(8,128)(2,1)} async-done(((bf16[1,2,64,768]{3,2,0,1:T(8,128)(2,1)}), bf16[1,2,512,768]{3,2,0,1:T(8,128)(2,1)}) %all-gather.44.cloned.1.call-update) | async-done | bytes 1572880 | tf_op jit(solution)/shard_map/all_gather | solution.py:364
  163.3 56.3 %all-gather.28.cloned.1.call-done = bf16[3,768,768]{2,1,0:T(8,128)(2,1)} async-done(((bf16[3,24,768]{2,1,0:T(8,128)(2,1)}), bf16[3,768,768]{2,1,0:T(8,128)(2,1)}) %all-gather.28.cloned.1.call-update) | async-done | bytes 3538960 | tf_op jit(solution)/shard_map/all_gather | solution.py:333
  221.4 95.8 %all-gather.30.cloned.1.call-done = bf16[2,2,768,2048]{3,2,1,0:T(8,128)(2,1)} async-done(((bf16[2,2,24,2048]{3,2,1,0:T(8,128)(2,1)}), bf16[2,2,768,2048]{3,2,1,0:T(8,128)(2,1)}) %all-gather.30.cloned.1.call-update) | async-done | bytes 12582928 | tf_op jit(solution)/shard_map/all_gather | solution.py:334
  321.0 66.7 %all-gather.32.cloned.1.call-done = bf16[2,2048,768]{2,1,0:T(8,128)(2,1)} async-done(((bf16[2,64,768]{2,1,0:T(8,128)(2,1)}), bf16[2,2048,768]{2,1,0:T(8,128)(2,1)}) %all-gather.32.cloned.1.call-update) | async-done | bytes 6291472 | tf_op jit(solution)/shard_map/all_gather | solution.py:335
  415.5 25.9 %all-gather.48.cloned.1.call-done = bf16[1,2,512,768]{3,2,0,1:T(8,128)(2,1)} async-done(((bf16[1,2,64,768]{3,2,0,1:T(8,128)(2,1)}), bf16[1,2,512,768]{3,2,0,1:T(8,128)(2,1)}) %all-gather.48.cloned.1.call-update) | async-done | bytes 1572880 | tf_op jit(solution)/shard_map/all_gather | solution.py:394
  456.1 13.5 all-gather.50.cloned.1.call-done
  476.9 20.2 %all-gather.52.cloned.1.call-done = bf16[1,2,512,768]{3,2,0,1:T(8,128)(2,1)} async-done(((bf16[1,2,64,768]{3,2,0,1:T(8,128)(2,1)}), bf16[1,2,512,768]{3,2,0,1:T(8,128)(2,1)}) %all-gather.52.cloned.1.call-update) | async-done | bytes 1572880 | tf_op jit(solution)/shard_map/all_gather | solution.py:421
  564.7 9.6 all_gather.89
  575.4 9.3 all_gather.87
  630.6 8.7 pad_maximum_fusion
  639.3 37.4 %copy.427 = f32[2,2,768,2048]{3,1,0,2:T(2,128)} copy(f32[2,2,768,2048]{2,3,1,0:T(8,128)} %pad_maximum_fusion) | data formatting | bytes 50331648 | tf_op jit(solution)/shard_map/stack | solution.py:632
  684.3 20.2 %tile.83 = f32[12,294975]{1,0:T(8,128)} reshape(f32[12,513,575]{2,1,0:T(8,128)} %tile.82) | data formatting | bytes 28317600 | tf_op jit(solution)/shard_map/while/body/eval_jaxpr/tile | solution.py:58
  704.5 15.1 slice.296
  719.6 21.1 %reshape.601 = f32[12,512,576]{2,1,0:T(8,128)} reshape(f32[12,294912]{1,0:T(8,128)} %slice.296) | data formatting | bytes 28311552 | tf_op jit(solution)/shard_map/while/body/eval_jaxpr/reshape | solution.py:59
  742.5 17.0 rev.31
  769.4 19.6 %tile.81 = f32[12,294975]{1,0:T(8,128)} reshape(f32[12,513,575]{2,1,0:T(8,128)} %tile.80) | data formatting | bytes 28317600 | tf_op jit(solution)/shard_map/while/body/eval_jaxpr/tile | solution.py:58
  789.1 14.7 slice.294
  803.7 21.9 %reshape.594 = f32[12,512,576]{2,1,0:T(8,128)} reshape(f32[12,294912]{1,0:T(8,128)} %slice.294) | data formatting | bytes 28311552 | tf_op jit(solution)/shard_map/while/body/eval_jaxpr/reshape | solution.py:59
  827.6 15.1 rev.30
  851.8 8.8 all_gather.95
  861.7 9.7 all_gather.91
  895.2 9.1 all_gather.97
  929.7 9.2 all_gather.93
  966.0 10.7 pad_maximum_fusion.1
  976.7 30.7 %copy.426 = f32[3,3,768,768]{3,1,0,2:T(4,128)} copy(f32[3,3,768,768]{2,3,1,0:T(8,128)} %pad_maximum_fusion.1) | data formatting | bytes 42467328 | tf_op jit(solution)/shard_map/stack | solution.py:630
  1014.1 8.8 pad_maximum_fusion.2
  1061.9 129.3 %all-reduce.19.cloned.1.call-done = f32[2,2,768,2048]{3,1,0,2:T(2,128)} async-done(((f32[2,2,768,2048]{3,1,0,2:T(2,128)}), f32[2,2,768,2048]{3,1,0,2:T(2,128)}) %all-reduce.19.cloned.1.call-update) | async-done | bytes 25165840
  1195.6 431.9 %all-reduce.17.cloned.1.call-done = f32[3,3,768,768]{3,1,0,2:T(4,128)} async-done(((f32[3,3,768,768]{3,1,0,2:T(4,128)}), f32[3,3,768,768]{3,1,0,2:T(4,128)}) %all-reduce.17.cloned.1.call-update) | async-done | bytes 21233680
  1631.4 158.0 %reduce-scatter.6.cloned.1.call-done = f32[2,64,768]{2,1,0:T(8,128)} async-done(((f32[2,2048,768]{2,1,0:T(8,128)}), f32[2,64,768]{2,1,0:T(8,128)}) %reduce-scatter.6.cloned.1.call-update) | async-done | bytes 393232 | tf_op jit(solution)/shard_map/reduce_scatter | solution.py:649
  1791.6 130.7 %all-reduce.21.cloned.1.call-done = (f32[7,768]{1,0:T(8,128)}, f32[2,32,12]{1,2,0:T(8,128)}, f32[3,3,768]{2,1,0:T(4,128)}, f32[3,768]{1,0:T(4,128)}, f32[2,2,2048]{2,1,0:T(2,128)}, /*index=5*/f32[2,768]{1,0:T(2,128)}) async-done(((f32[7,768]{1,0:T(8,128)}, f32[2,32,12]{1,2,0:T(8,128)}, f32[3,3,768]{2,1,0:T(4,128)}, f32[3,768]{1,0:T(4,128)}, f32[2,2,2048]{2,1,0:T(2,128)}, /*index=5*/f32[2,768]{1,0:T(2,128)}), ...) | async-done | bytes 100368
  (717 shorter events, 382.9 us)
Async XLA Ops:
  7.2 93.8 %all-gather.26.cloned.1.call-start = ((), (), s32[]{:S(2)}) async-start(), calls=%async_computation.2 | async-start | bytes 10948608 | tf_op jit(solution)/shard_map/all_gather | solution.py:332
  7.9 121.1 %all-gather.42.cloned.1.call-start = ((), (), s32[]{:S(2)}) async-start(), calls=%async_computation.12 | async-start | bytes 1769472 | tf_op jit(solution)/shard_map/all_gather | solution.py:363
  52.9 51.8 %copy-start.134 = (f32[768]{0:T(1024)}, f32[768]{0:T(1024)S(1)}, u32[]{:S(2)}) copy-start(f32[768]{0:T(1024)S(1)} %get-tuple-element.469) | copy-start | bytes 9220
  52.9 54.5 %copy-start.136 = (f32[768]{0:T(1024)}, f32[768]{0:T(1024)S(1)}, u32[]{:S(2)}) copy-start(f32[768]{0:T(1024)S(1)} %get-tuple-element.466) | copy-start | bytes 9220
  52.9 264.3 %copy-start.124 = (f32[768]{0:T(1024)}, f32[768]{0:T(1024)S(1)}, u32[]{:S(2)}) copy-start(f32[768]{0:T(1024)S(1)} %get-tuple-element.468) | copy-start | bytes 9220
  52.9 337.7 %copy-start.141 = (f32[768]{0:T(1024)}, f32[768]{0:T(1024)S(1)}, u32[]{:S(2)}) copy-start(f32[768]{0:T(1024)S(1)} %get-tuple-element.467) | copy-start | bytes 9220
  52.9 400.1 %copy-start.138 = (f32[768]{0:T(1024)}, f32[768]{0:T(1024)S(1)}, u32[]{:S(2)}) copy-start(f32[768]{0:T(1024)S(1)} %get-tuple-element.465) | copy-start | bytes 9220
  104.7 51.9 %all-gather.44.cloned.1.call-start = ((), (), s32[]{:S(2)}) async-start(), calls=%async_computation.13 | async-start | bytes 1769472 | tf_op jit(solution)/shard_map/all_gather | solution.py:364
  105.4 114.2 %all-gather.28.cloned.1.call-start = ((), (), s32[]{:S(2)}) async-start(), calls=%async_computation.3 | async-start | bytes 3649536 | tf_op jit(solution)/shard_map/all_gather | solution.py:333
  106.0 211.1 %all-gather.30.cloned.1.call-start = ((), (), s32[]{:S(2)}) async-start(), calls=%async_computation.4 | async-start | bytes 12976128 | tf_op jit(solution)/shard_map/all_gather | solution.py:334
  106.6 281.1 %all-gather.32.cloned.1.call-start = ((), (), s32[]{:S(2)}) async-start(), calls=%async_computation.5 | async-start | bytes 6488064 | tf_op jit(solution)/shard_map/all_gather | solution.py:335
  107.2 306.6 %all-gather.46.cloned.1.call-start = ((), (), s32[]{:S(2)}) async-start(), calls=%async_computation.14 | async-start | bytes 1769472 | tf_op jit(solution)/shard_map/all_gather | solution.py:393
  111.0 330.4 %all-gather.48.cloned.1.call-start = ((), (), s32[]{:S(2)}) async-start(), calls=%async_computation.15 | async-start | bytes 1769472 | tf_op jit(solution)/shard_map/all_gather | solution.py:394
  111.6 284.1 %copy-start.173 = (s32[64]{0:T(128)}, s32[64]{0:T(128)S(1)}, u32[]{:S(2)}) copy-start(s32[64]{0:T(128)S(1)} %iota_add_fusion) | copy-start | bytes 772
  124.9 344.8 %all-gather.50.cloned.1.call-start = ((), (), s32[]{:S(2)}) async-start(), calls=%async_computation.16 | async-start | bytes 1769472 | tf_op jit(solution)/shard_map/all_gather | solution.py:420
  158.4 61.2 %copy-start.64 = (bf16[2,64,768]{2,1,0:T(8,128)(2,1)S(1)}, bf16[2,64,768]{2,1,0:T(8,128)(2,1)}, u32[]{:S(2)}) copy-start(bf16[2,64,768]{2,1,0:T(8,128)(2,1)} %param.14) | copy-start | bytes 589828
  221.3 99.7 %copy-start.182 = (f32[2,64]{1,0:T(2,128)}, f32[2,64]{1,0:T(2,128)S(1)}, u32[]{:S(2)}) copy-start(f32[2,64]{1,0:T(2,128)S(1)} %get-tuple-element.513) | copy-start | bytes 1540
  221.3 166.4 %copy-start.46 = (f32[2,64,768]{2,1,0:T(8,128)}, f32[2,64,768]{2,1,0:T(8,128)S(1)}, u32[]{:S(2)}) copy-start(f32[2,64,768]{2,1,0:T(8,128)S(1)} %get-tuple-element.514) | copy-start | bytes 1179652
  221.3 99.7 %copy-start.147 = (f32[2,64]{1,0:T(2,128)}, f32[2,64]{1,0:T(2,128)S(1)}, u32[]{:S(2)}) copy-start(f32[2,64]{1,0:T(2,128)S(1)} %fusion.277) | copy-start | bytes 1540
  321.0 69.4 %copy-start.6 = (f32[2,2,64,2048]{3,2,0,1:T(8,128)}, f32[2,2,64,2048]{3,2,0,1:T(8,128)S(1)}, u32[]{:S(2)}) copy-start(f32[2,2,64,2048]{3,2,0,1:T(8,128)S(1)} %fusion.17) | copy-start | bytes 6291460
  394.9 102.2 %all-gather.52.cloned.1.call-start = ((), (), s32[]{:S(2)}) async-start(), calls=%async_computation.17 | async-start | bytes 1769472 | tf_op jit(solution)/shard_map/all_gather | solution.py:421
  396.4 144.0 %all-gather.34.cloned.1.call-start = ((), (), s32[]{:S(2)}) async-start(), calls=%async_computation.6 | async-start | bytes 1769472 | tf_op jit(solution)/shard_map/all_gather | solution.py:514
  455.9 135.0 %all-gather.36.cloned.1.call-start = ((), (), s32[]{:S(2)}) async-start(), calls=%async_computation.7 | async-start | bytes 1769472 | tf_op jit(solution)/shard_map/all_gather | solution.py:515
  531.5 340.9 %all-gather.56.cloned.1.call-start = ((), (), s32[]{:S(2)}) async-start(), calls=%async_computation.19 | async-start | bytes 1769472 | tf_op jit(solution)/shard_map/all_gather | solution.py:537
  532.3 341.9 %all-gather.54.cloned.1.call-start = ((), (), s32[]{:S(2)}) async-start(), calls=%async_computation.18 | async-start | bytes 1769472 | tf_op jit(solution)/shard_map/all_gather | solution.py:608
  532.9 377.4 %all-gather.40.cloned.1.call-start = ((), (), s32[]{:S(2)}) async-start(), calls=%async_computation.9 | async-start | bytes 1769472 | tf_op jit(solution)/shard_map/all_gather | solution.py:538
  590.7 357.6 %all-gather.38.cloned.1.call-start = ((), (), s32[]{:S(2)}) async-start(), calls=%async_computation.8 | async-start | bytes 1769472 | tf_op jit(solution)/shard_map/all_gather | solution.py:609
  620.2 439.4 %reduce-scatter.4.cloned.1.call-start = ((), (), s32[]{:S(2)}) async-start(), calls=%async_computation.10 | async-start | bytes 7299072 | tf_op jit(solution)/shard_map/reduce_scatter | solution.py:647
  625.2 566.1 %all-reduce.19.cloned.1.call-start = ((), (), s32[]{:S(2)}) async-start(), calls=%async_computation.21 | async-start | bytes 50331648
  676.7 950.8 %all-reduce.17.cloned.1.call-start = ((), (), s32[]{:S(2)}) async-start(), calls=%async_computation.20 | async-start | bytes 56623104
  1007.4 781.9 %reduce-scatter.6.cloned.1.call-start = ((), (), s32[]{:S(2)}) async-start(), calls=%async_computation.11 | async-start | bytes 12976128 | tf_op jit(solution)/shard_map/reduce_scatter | solution.py:649
  1022.9 899.5 %all-reduce.21.cloned.1.call-start = ((), (), s32[]{:S(2)}) async-start(), calls=%async_computation.22 | async-start | bytes 258048
  (192 other events, 1434.5 us)
Sparse Core Ops, SparseCore 0:
  11.0 89.9 all-gather.25
  104.8 24.1 all-gather.41
  130.9 25.6 all-gather.43
  159.4 60.1 all-gather.27
  222.3 94.8 all-gather.29
  319.8 67.7 all-gather.31
  389.6 24.1 all-gather.45
  415.7 25.6 all-gather.47
  443.9 25.6 all-gather.49
  471.4 25.6 all-gather.51
  499.0 25.6 all-gather.33
  531.7 25.9 all-gather.35
  559.5 27.2 all-gather.55
  588.5 25.7 all-gather.53
  616.1 25.7 all-gather.39
  643.6 25.6 all-gather.37
  675.4 119.1 reduce-scatter.3
  801.9 389.2 all-reduce.18
  1198.8 428.6 all-reduce.16
  1634.0 155.3 reduce-scatter.5
  1798.0 124.2 all-reduce.20
where the time goes:
time: 1950 us; the launch traced here: 1940 us
  waiting for transfers between devices  1210 us (62%)
  local copies, waits for them, and re-layouts  369 us (19%)
  matrix products  158 us (8%)
  blocking collectives  99.6 us (5%)
  other arithmetic  79.9 us (4%)
    unnamed x24, waiting for transfers between devices  696 us
    reduce_scatter x1, waiting for transfers between devices, local(): lax.psum_scatter(grad_hidden_out, ('dp', 'seq'), scatter_dimension=1, til...  158 us
    all_gather x1, waiting for transfers between devices, local(): lax.all_gather(hidden_in, ('dp', 'seq'), axis=2, tiled=True)  95.8 us
    all_gather x1, waiting for transfers between devices, local(): lax.all_gather(hidden_out, ('dp', 'seq'), axis=1, tiled=True)  66.7 us
    another operation x8, local copies, waits for them, and re-layouts, hankel_block(): tiled = jnp.tile(window, (1, rows + 1))[:, :rows * (length + 1)]  60.7 us
    all_gather x1, waiting for transfers between devices, local(): lax.all_gather(attention_out, ('dp', 'seq'), axis=1, tiled=True)  56.3 us
    reshape x6, local copies, waits for them, and re-layouts, hankel_block(): return tiled.reshape(heads_here, rows, length + 1)[:, :, :cols]  52.4 us
    all_gather x1, waiting for transfers between devices, local(): lax.all_gather(attention_in, ('dp', 'seq'), axis=2, tiled=True)  47 us
  transfers between devices with their start and end apart: 21, of which 14 were waited for; matrix products, arithmetic and copies ran while one was open for 30% of the time, Pallas kernels for 0%

commit v1 on v0

--- a/solution.py
+++ b/solution.py
@@ -1,8 +1,11 @@
+import functools
 import math
 
 import jax
 import jax.numpy as jnp
 from jax import lax
+from jax.experimental import pallas as pl
+from jax.experimental.pallas import tpu as pltpu
 from jax.sharding import PartitionSpec as P
 
 D = 768
@@ -692,9 +695,567 @@
     )
 
 
+WAYS = 4
+
+
+def swap(values, bits):
+    return lax.ppermute(values, "seq", [(s, s ^ bits) for s in range(8)])
+
+
+def swap_core(values):
+    return swap(values, 1)
+
+
+def swap_x(values):
+    return swap(values, 2)
+
+
+def swap_y(values):
+    return swap(values, 4)
+
+
+def shift_z(values, hops, count):
+    return lax.ppermute(values, "dp", [(i, (i + hops) % count) for i in range(count)])
+
+
+def pair_up(mine, other, bit):
+    first = bit == 0
+    return jnp.stack([jnp.where(first, mine, other), jnp.where(first, other, mine)])
+
+
+def pick(values, index, axis=0):
+    return lax.dynamic_index_in_dim(values, index, axis, keepdims=False)
+
+
+class Place:
+    def __init__(self, depth):
+        self.depth = depth
+        self.z = lax.axis_index("dp")
+        s = lax.axis_index("seq")
+        self.y, self.x, self.c = s // 4, (s // 2) % 2, s % 2
+        self.q = s % 4
+
+
+def exchange_columns(place, pieces):
+    halves = pieces.reshape((2, 2) + pieces.shape[1:])
+    got = swap_x(pick(halves, 1 - place.x))
+    both = pair_up(pick(halves, place.x), got, place.x)
+    got = swap_core(pick(both, 1 - place.c, 1))
+    whole = pair_up(pick(both, place.c, 1), got, place.c)
+    return jnp.swapaxes(whole, 0, 1).reshape(pieces.shape)
+
+
+def gather_rows(place, piece):
+    depth = place.depth
+    held = jnp.zeros((depth,) + piece.shape, piece.dtype)
+    arrivals = [(0, piece)] + [(k, shift_z(piece, k, depth)) for k in range(1, depth)]
+    for hops, block in arrivals:
+        held = lax.dynamic_update_index_in_dim(held, block, (place.z - hops) % depth, 0)
+    other = swap_y(held)
+    first = place.y == 0
+    return jnp.stack([jnp.where(first, held, other), jnp.where(first, other, held)], axis=1)
+
+
+def scatter_rows(place, parts):
+    depth = place.depth
+    sent = swap_y(rounded(pick(parts, 1 - place.y, 1)))
+    halves = pick(parts, place.y, 1) + sent.astype(jnp.float32)
+    halves_low = rounded(halves)
+    total = pick(halves, place.z)
+    for hops in range(1, depth):
+        total = total + shift_z(pick(halves_low, (place.z + hops) % depth), hops, depth).astype(
+            jnp.float32
+        )
+    return total
+
+
+def turn(values, depth, back=False):
+    pairs = []
+    for d in range(depth):
+        for y in range(2):
+            for q in range(WAYS):
+                pairs.append((d * 8 + y * 4 + q, q * 8 + y * 4 + d))
+    return lax.ppermute(values, ("dp", "seq"), pairs)
+
+
+def sum_group(place, partial):
+    half = partial.shape[0] // 2
+    parts = partial.reshape(2, half, partial.shape[1])
+    chip = pick(parts, place.c) + swap_core(rounded(pick(parts, 1 - place.c))).astype(jnp.float32)
+    return chip + swap_x(rounded(chip)).astype(jnp.float32)
+
+
+def both_cores(place, half):
+    whole = pair_up(half, swap_core(half), place.c)
+    return whole.reshape((2 * half.shape[0],) + half.shape[1:])
+
+
+def matmul(a, b):
+    return jnp.dot(a, b, preferred_element_type=jnp.float32)
+
+
+def matmul_nt(a, b):
+    return lax.dot_general(a, b, (((1,), (1,)), ((), ())), preferred_element_type=jnp.float32)
+
+
+def matmul_tn(a, b):
+    return lax.dot_general(a, b, (((0,), (0,)), ((), ())), preferred_element_type=jnp.float32)
+
+
+def inner_block(block):
+    y, x, c = block // 4, (block // 2) % 2, block % 2
+    return c * 4 + y * 2 + x
+
+
+def in_order(ref, first, width):
+    step = ref.shape[0] // 8
+    return jnp.concatenate(
+        [
+            ref[inner_block(n) * step : (inner_block(n) + 1) * step, first : first + width]
+            for n in range(8)
+        ],
+        axis=0,
+    )
+
+
+def out_of_order(ref, first, values):
+    step = ref.shape[0] // 8
+    for n in range(8):
+        at = inner_block(n)
+        ref[at * step : (at + 1) * step, first : first + values.shape[1]] = values[
+            n * step : (n + 1) * step
+        ].astype(ref.dtype)
+
+
+TILE = 128
+
+
+def attend_kernel(heads, causal, biased, *refs):
+    if biased:
+        length_ref, q_ref, kv_ref, table_ref, ctx_ref, p_ref = refs
+    else:
+        length_ref, q_ref, kv_ref, ctx_ref, p_ref = refs
+    rows = q_ref.shape[0]
+    tiles = rows // TILE
+    length = length_ref[0]
+    width = heads * HEAD
+    cols = lax.broadcasted_iota(jnp.int32, (TILE, rows), 1)
+    for h in range(heads):
+        q = in_order(q_ref, h * HEAD, HEAD)
+        k = in_order(kv_ref, kv_ref.shape[1] - 2 * width + h * HEAD, HEAD)
+        v = in_order(kv_ref, kv_ref.shape[1] - width + h * HEAD, HEAD)
+        if biased:
+            line = jnp.broadcast_to(table_ref[h : h + 1, :], (TILE, 2 * rows))
+            skew = pltpu.roll(line, 2 * rows - (TILE - 1), 1, stride=1, stride_axis=0)
+        contexts = []
+        for i in range(tiles):
+            s = matmul_nt(q[i * TILE : (i + 1) * TILE], k) * (HEAD**-0.5)
+            if biased:
+                begin = (tiles - 1 - i) * TILE
+                s = s + skew[:, begin : begin + rows]
+            visible = cols < length
+            if causal:
+                ids = lax.broadcasted_iota(jnp.int32, (TILE, rows), 0) + i * TILE
+                visible = visible & (cols <= ids)
+            s = jnp.where(visible, s, NEGATIVE)
+            e = jnp.exp(s - jnp.max(s, axis=-1, keepdims=True))
+            p = (e / jnp.sum(e, axis=-1, keepdims=True)).astype(jnp.bfloat16)
+            p_ref[h, i * TILE : (i + 1) * TILE, :] = p
+            contexts.append(matmul(p, v))
+        out_of_order(ctx_ref, h * HEAD, jnp.concatenate(contexts, axis=0))
+
+
+def attend_local(q, kv, table, length, causal):
+    rows = q.shape[0]
+    heads = HEADS // WAYS
+    biased = table is not None
+    vmem = pl.BlockSpec(memory_space=pltpu.VMEM)
+    operands = [length.reshape(1), q, kv] + ([table] if biased else [])
+    return pl.pallas_call(
+        functools.partial(attend_kernel, heads, causal, biased),
+        out_shape=(
+            jax.ShapeDtypeStruct((rows, heads * HEAD), jnp.float32),
+            jax.ShapeDtypeStruct((heads, rows, rows), jnp.bfloat16),
+        ),
+        in_specs=[pl.BlockSpec(memory_space=pltpu.SMEM)] + [vmem] * (len(operands) - 1),
+        out_specs=(vmem, vmem),
+        compiler_params=pltpu.CompilerParams(vmem_limit_bytes=40 * 2**20),
+        cost_estimate=pl.CostEstimate(
+            flops=4 * heads * rows * rows * HEAD,
+            bytes_accessed=2 * heads * rows * (rows + 5 * HEAD),
+            transcendentals=heads * rows * rows,
+        ),
+        name="attend",
+    )(*operands)
+
+
+def attend_back_kernel(heads, biased, *refs):
+    if biased:
+        q_ref, kv_ref, p_ref, ctx_ref, g_ref, dqkv_ref, dtable_ref, ds_ref = refs
+    else:
+        q_ref, kv_ref, p_ref, ctx_ref, g_ref, dqkv_ref, ds_ref = refs
+    rows = q_ref.shape[0]
+    tiles = rows // TILE
+    width = heads * HEAD
+    factor = HEAD**-0.5
+    for h in range(heads):
+        q = in_order(q_ref, h * HEAD, HEAD)
+        k = in_order(kv_ref, kv_ref.shape[1] - 2 * width + h * HEAD, HEAD)
+        v = in_order(kv_ref, kv_ref.shape[1] - width + h * HEAD, HEAD)
+        g = in_order(g_ref, h * HEAD, HEAD)
+        context = in_order(ctx_ref, h * HEAD, HEAD)
+        dots = jnp.sum(g.astype(jnp.float32) * context, axis=-1, keepdims=True)
+        if biased:
+            sums = [None] * (2 * tiles - 1)
+        for i in range(tiles):
+            at = slice(i * TILE, (i + 1) * TILE)
+            dp = matmul_nt(g[at], v)
+            ds = p_ref[h, at, :].astype(jnp.float32) * (dp - dots[at])
+            if biased:
+                for j in range(tiles):
+                    slot = tiles - 1 - i + j
+                    part = ds[:, j * TILE : (j + 1) * TILE]
+                    sums[slot] = part if sums[slot] is None else sums[slot] + part
+            ds_ref[at, :] = (ds * factor).astype(jnp.bfloat16)
+        ds_low = ds_ref[...]
+        out_of_order(dqkv_ref, h * HEAD, matmul(ds_low, k))
+        out_of_order(dqkv_ref, width + h * HEAD, matmul_tn(ds_low, q))
+        out_of_order(dqkv_ref, 2 * width + h * HEAD, matmul_tn(p_ref[h], g))
+        if biased:
+            band = jnp.concatenate(sums + [jnp.zeros((TILE, TILE), jnp.float32)], axis=1)
+            ids = lax.broadcasted_iota(jnp.int32, band.shape, 0)
+            bit = 1
+            while bit < TILE:
+                moved = pltpu.roll(band, 2 * rows - bit, 1)
+                band = jnp.where((ids & bit) != 0, moved, band)
+                bit *= 2
+            line = jnp.sum(band, axis=0, keepdims=True)
+            dtable_ref[h : h + 1, :] = pltpu.roll(line, TILE - 1, 1)
+
+
+def attend_local_back(q, kv, p, ctx, g, biased):
+    rows = q.shape[0]
+    heads = HEADS // WAYS
+    vmem = pl.BlockSpec(memory_space=pltpu.VMEM)
+    shapes = [jax.ShapeDtypeStruct((rows, 3 * heads * HEAD), jnp.bfloat16)]
+    if biased:
+        shapes.append(jax.ShapeDtypeStruct((heads, 2 * rows), jnp.float32))
+    result = pl.pallas_call(
+        functools.partial(attend_back_kernel, heads, biased),
+        out_shape=tuple(shapes),
+        in_specs=[vmem] * 5,
+        out_specs=(vmem,) * len(shapes),
+        scratch_shapes=[pltpu.VMEM((rows, rows), jnp.bfloat16)],
+        compiler_params=pltpu.CompilerParams(vmem_limit_bytes=40 * 2**20),
+        cost_estimate=pl.CostEstimate(
+            flops=8 * heads * rows * rows * HEAD,
+            bytes_accessed=2 * heads * rows * (rows + 8 * HEAD),
+            transcendentals=0,
+        ),
+        name="attend_back",
+    )(q, kv, p, ctx, g)
+    return result if biased else (result[0], None)
+
+
+def gather_own_rows(place, mine, other_seq):
+    near = pair_up(mine, swap_y(other_seq), place.y)
+    far = pair_up(near, swap_x(near), place.x)
+    far = far.transpose(2, 1, 0, 3, 4)
+    return far.reshape(far.shape[0], -1, far.shape[4])
+
+
+def give_back(place, half):
+    blocks = half.reshape(2, 2, -1, half.shape[1])
+    blocks = pick(blocks, place.x, 1)
+    other = swap_y(pick(blocks, 1 - place.y))
+    return pair_up(pick(blocks, place.y), other, place.y)
+
+
+def group_feed_back(place, residual, gain, weights_in, weights_out, kept, upstream):
+    normed, gate, up, hidden = kept
+    up_low = both_cores(place, rounded(upstream))
+    grad_hidden = matmul_nt(up_low, weights_out)
+    _, pullback = jax.vjp(lambda a, b: jax.nn.gelu(a, approximate=True) * b, gate, up)
+    grad_gate, grad_up = pullback(grad_hidden)
+    grad_gate_up = jnp.concatenate([rounded(grad_gate), rounded(grad_up)], axis=1)
+    grad_normed = sum_group(place, matmul_nt(grad_gate_up, weights_in))
+    grad_out = matmul_tn(hidden, up_low)
+    grad_in = matmul_tn(normed, grad_gate_up)
+    grad_residual, grad_gain = rms_back(residual, gain, grad_normed)
+    return (upstream + grad_residual, grad_gain, grad_in, grad_out)
+
+
+def group_feed_forward(place, residual, gain, weights_in, weights_out):
+    normed = both_cores(place, rounded(rms_norm(residual, gain)))
+    gate_up = matmul(normed, weights_in)
+    gate, up = jnp.split(gate_up, 2, axis=1)
+    hidden = rounded(jax.nn.gelu(gate, approximate=True) * up)
+    output = sum_group(place, matmul(hidden, weights_out))
+    return (residual + output, (normed, gate, up, hidden))
+
+
+def sum_everywhere(place, values):
+    depth = place.depth
+    for bits in (1, 2, 4):
+        values = values + swap(values, bits)
+    return values + sum(shift_z(values, k, depth) for k in range(1, depth))
+
+
+def split_columns(weights):
+    pieces = weights.reshape(weights.shape[:-1] + (WAYS, -1))
+    return jnp.moveaxis(pieces, -2, 0)
+
+
+def grouped(
+    depth,
+    enc_input,
+    dec_input,
+    enc_lengths,
+    dec_lengths,
+    enc_buckets,
+    dec_buckets,
+    attention_in,
+    attention_out,
+    hidden_in,
+    hidden_out,
+    norm_gains,
+    position_bias,
+    enc_cotangent,
+    dec_cotangent,
+):
+    place = Place(depth)
+    y, q = place.y, place.q
+    length = enc_input.shape[1] * 8
+    own = attention_in.shape[2]
+    ff_own = hidden_out.shape[1]
+    ff = ff_own * 2 * depth
+    heads = HEADS // WAYS
+    width = heads * HEAD
+
+    in_pieces = split_columns(attention_in)
+    in_pieces = in_pieces.transpose(0, 1, 3, 2, 4).reshape(WAYS, 3, own, 3 * width)
+    enc_piece = exchange_columns(place, in_pieces[:, 0]).reshape(WAYS * own, 3 * width)
+    w_enc = gather_rows(place, enc_piece).reshape(D, 3 * width)
+    turned = turn(attention_out, depth)
+    w_out_enc = gather_rows(place, turned[0])
+    hidden_pieces = hidden_in.reshape(2, 2, own, 2 * depth, WAYS, ff_own)
+    hidden_pieces = hidden_pieces.transpose(4, 0, 2, 1, 3, 5).reshape(WAYS, 2, own, 2 * ff)
+    hid_enc = exchange_columns(place, hidden_pieces[:, 0]).reshape(WAYS * own, 2 * ff)
+    w_hin_enc = gather_rows(place, hid_enc).reshape(D, 2 * ff)
+    w_hout_enc = gather_rows(place, hidden_out[0]).reshape(ff, D)
+    rest = exchange_columns(place, in_pieces[:, 1:])
+    rest = rest.transpose(1, 0, 2, 3).reshape(2 * WAYS * own, 3 * width)
+    w_rest = gather_rows(place, rest).reshape(2 * depth, 2, WAYS * own, 3 * width)
+    w_dec = w_rest[:, 0].reshape(D, 3 * width)
+    w_cross = w_rest[:, 1].reshape(D, 3 * width)
+    w_out_rest = gather_rows(place, turned[1:])
+    hid_dec = exchange_columns(place, hidden_pieces[:, 1]).reshape(WAYS * own, 2 * ff)
+    w_hin_dec = gather_rows(place, hid_dec).reshape(D, 2 * ff)
+    w_hout_dec = gather_rows(place, hidden_out[1]).reshape(ff, D)
+
+    def out_rows(gathered):
+        return gathered.transpose(1, 0, 2, 3).reshape(width, D)
+
+    w_out_enc = out_rows(w_out_enc)
+    w_out_dec, w_out_cross = out_rows(w_out_rest[:, :, 0]), out_rows(w_out_rest[:, :, 1])
+    gains_full = lax.all_gather(norm_gains, ("dp", "seq"), axis=1, tiled=True)
+    gains = gains_full.astype(jnp.float32)
+
+    def mine_other(array):
+        return (pick(array, y), pick(array, 1 - y))
+
+    enc_mine, enc_other = mine_other(enc_input)
+    dec_mine, dec_other = mine_other(dec_input)
+    enc_half = gather_own_rows(place, enc_mine[None], enc_other[None])[0]
+    enc_full = both_cores(place, enc_half)
+    dec_half = gather_own_rows(place, dec_mine[None], dec_other[None])[0]
+    dec_full = both_cores(place, dec_half)
+    cot_mine = jnp.stack([pick(dec_cotangent, y), pick(enc_cotangent, y)])
+    cot_other = jnp.stack([pick(dec_cotangent, 1 - y), pick(enc_cotangent, 1 - y)])
+    cots = gather_own_rows(place, cot_mine, cot_other).astype(jnp.float32)
+    enc_length = pick(enc_lengths, y)
+    dec_length = pick(dec_lengths, y)
+
+    enc_table = offset_table(enc_buckets, position_bias[0])
+    enc_table = jnp.pad(enc_table, ((0, 0), (0, 1)))
+    dec_table = offset_table(dec_buckets, position_bias[1])
+    dec_table = jnp.concatenate(
+        [dec_table[:, ::-1], jnp.broadcast_to(dec_table[:, :1], (HEADS, length))], axis=1
+    )
+    enc_table = lax.dynamic_slice_in_dim(enc_table, q * heads, heads, 0)
+    dec_table = lax.dynamic_slice_in_dim(dec_table, q * heads, heads, 0)
+
+    enc_values = enc_half.astype(jnp.float32)
+    norm_a = rounded(rms_norm(enc_full.astype(jnp.float32), gains[0]))
+    qkv_enc = rounded(matmul(norm_a, w_enc))
+    ctx_enc, p_enc = attend_local(qkv_enc, qkv_enc, enc_table, enc_length, False)
+    ctx_enc_low = rounded(ctx_enc)
+    enc_mid = enc_values + sum_group(place, matmul(ctx_enc_low, w_out_enc))
+    enc_last, enc_kept = group_feed_forward(place, enc_mid, gains[1], w_hin_enc, w_hout_enc)
+    memory = rms_norm(enc_last, gains[2])
+    memory_low = both_cores(place, rounded(memory))
+
+    dec_values = dec_half.astype(jnp.float32)
+    norm_b = rounded(rms_norm(dec_full.astype(jnp.float32), gains[3]))
+    qkv_dec = rounded(matmul(norm_b, w_dec))
+    ctx_dec, p_dec = attend_local(qkv_dec, qkv_dec, dec_table, dec_length, True)
+    ctx_dec_low = rounded(ctx_dec)
+    dec_mid = dec_values + sum_group(place, matmul(ctx_dec_low, w_out_dec))
+    norm_c = both_cores(place, rounded(rms_norm(dec_mid, gains[4])))
+    q_cross = rounded(matmul(norm_c, w_cross[:, :width]))
+    kv_cross = rounded(matmul(memory_low, w_cross[:, width:]))
+    ctx_cross, p_cross = attend_local(q_cross, kv_cross, None, enc_length, False)
+    ctx_cross_low = rounded(ctx_cross)
+    dec_cross = dec_mid + sum_group(place, matmul(ctx_cross_low, w_out_cross))
+    dec_last, dec_kept = group_feed_forward(place, dec_cross, gains[5], w_hin_dec, w_hout_dec)
+    dec_final = rms_norm(dec_last, gains[6])
+
+    g_dec_last, gg6 = rms_back(dec_last, gains[6], cots[0])
+    g_dec_cross, gg5, d_hin_dec, d_hout_dec = group_feed_back(
+        place, dec_cross, gains[5], w_hin_dec, w_hout_dec, dec_kept, g_dec_last
+    )
+    up_low = both_cores(place, rounded(g_dec_cross))
+    g_ctx = rounded(matmul_nt(up_low, w_out_cross))
+    d_out_cross = matmul_tn(ctx_cross_low, up_low)
+    dqkv_cross, _ = attend_local_back(q_cross, kv_cross, p_cross, ctx_cross, g_ctx, False)
+    g_memory = cots[1] + sum_group(place, matmul_nt(dqkv_cross[:, width:], w_cross[:, width:]))
+    g_norm_c = sum_group(place, matmul_nt(dqkv_cross[:, :width], w_cross[:, :width]))
+    d_cross = jnp.concatenate(
+        [
+            matmul_tn(norm_c, dqkv_cross[:, :width]),
+            matmul_tn(memory_low, dqkv_cross[:, width:]),
+        ],
+        axis=1,
+    )
+    g_part, gg4 = rms_back(dec_mid, gains[4], g_norm_c)
+    g_dec_mid = g_dec_cross + g_part
+    up_low = both_cores(place, rounded(g_dec_mid))
+    g_ctx = rounded(matmul_nt(up_low, w_out_dec))
+    d_out_dec = matmul_tn(ctx_dec_low, up_low)
+    dqkv_dec, d_table_dec = attend_local_back(qkv_dec, qkv_dec, p_dec, ctx_dec, g_ctx, True)
+    g_norm_b = sum_group(place, matmul_nt(dqkv_dec, w_dec))
+    d_dec = matmul_tn(norm_b, dqkv_dec)
+    g_part, gg3 = rms_back(dec_values, gains[3], g_norm_b)
+    grad_dec_half = g_dec_mid + g_part
+
+    g_enc_last, gg2 = rms_back(enc_last, gains[2], g_memory)
+    g_enc_mid, gg1, d_hin_enc, d_hout_enc = group_feed_back(
+        place, enc_mid, gains[1], w_hin_enc, w_hout_enc, enc_kept, g_enc_last
+    )
+    up_low = both_cores(place, rounded(g_enc_mid))
+    g_ctx = rounded(matmul_nt(up_low, w_out_enc))
+    d_out_enc = matmul_tn(ctx_enc_low, up_low)
+    dqkv_enc, d_table_enc = attend_local_back(qkv_enc, qkv_enc, p_enc, ctx_enc, g_ctx, True)
+    g_norm_a = sum_group(place, matmul_nt(dqkv_enc, w_enc))
+    d_enc = matmul_tn(norm_a, dqkv_enc)
+    g_part, gg0 = rms_back(enc_values, gains[0], g_norm_a)
+    grad_enc_half = g_enc_mid + g_part
+
+    def in_parts(grads):
+        return grads.reshape(depth, 2, WAYS * own, grads.shape[1])
+
+    def out_parts(grads):
+        return grads.reshape(2, depth, own, D).transpose(1, 0, 2, 3)
+
+    def to_rows(shard):
+        return exchange_columns(place, rounded(shard).reshape(WAYS, own, -1)).astype(jnp.float32)
+
+    shard_hin_dec = to_rows(scatter_rows(place, in_parts(d_hin_dec)))
+    shard_hout_dec = scatter_rows(place, d_hout_dec.reshape(depth, 2, ff_own, D))
+    shard_cross = to_rows(scatter_rows(place, in_parts(d_cross)))
+    shard_dec = to_rows(scatter_rows(place, in_parts(d_dec)))
+    shard_hin_enc = to_rows(scatter_rows(place, in_parts(d_hin_enc)))
+    shard_hout_enc = scatter_rows(place, d_hout_enc.reshape(depth, 2, ff_own, D))
+    outs = [scatter_rows(place, out_parts(g)) for g in (d_out_cross, d_out_dec, d_out_enc)]
+    shard_enc = to_rows(scatter_rows(place, in_parts(d_enc)))
+    shard_out = turn(rounded(jnp.stack(outs[::-1])), depth).astype(jnp.float32)
+    shard_out = jnp.stack([shard_out[0], shard_out[1], shard_out[2]])
+    shard_in = jnp.stack([shard_enc, shard_dec, shard_cross])
+    shard_in = shard_in.reshape(3, WAYS, own, 3, width).transpose(0, 3, 2, 1, 4)
+    shard_in = shard_in.reshape(3, 3, own, D)
+    shard_hin = jnp.stack([shard_hin_enc, shard_hin_dec])
+    shard_hin = shard_hin.reshape(2, WAYS, own, 2, 2 * depth, ff_own).transpose(0, 3, 2, 4, 1, 5)
+    shard_hin = shard_hin.reshape(2, 2, own, WAYS * ff)
+    shard_hout = jnp.stack([shard_hout_enc, shard_hout_dec])
+
+    buckets = position_bias.shape[1]
+    grad_enc_bias = d_table_enc[:, : 2 * length - 1]
+    grad_dec_bias = d_table_dec[:, :length][:, ::-1]
+    grad_position = jnp.stack(
+        [
+            bucket_grad(enc_buckets, grad_enc_bias, buckets),
+            bucket_grad(dec_buckets, grad_dec_bias, buckets),
+        ]
+    )
+    grad_position = lax.dynamic_update_slice_in_dim(
+        jnp.zeros_like(position_bias), grad_position, q * heads, 2
+    )
+    grad_gains = jnp.stack([gg0, gg1, gg2, gg3, gg4, gg5, gg6])
+    grad_gains = jnp.where(place.x == 0, grad_gains, 0.0)
+    small = jnp.concatenate([grad_gains.reshape(-1, 128), grad_position.reshape(-1, 128)])
+    small = sum_everywhere(place, small)
+    cut = grad_gains.size // 128
+    grad_gains = small[:cut].reshape(grad_gains.shape)
+    grad_position = small[cut:].reshape(grad_position.shape)
+    shard_gains = lax.dynamic_slice_in_dim(
+        grad_gains, (place.z * 8 + lax.axis_index("seq")) * own, own, 1
+    )
+
+    squares = [v * v for v in (shard_in, shard_out, shard_hin, shard_hout)]
+    columns = [jnp.sum(v, axis=-2) for v in squares]
+    flat = sum_everywhere(place, jnp.concatenate([v.reshape(-1, 128) for v in columns]))
+    totals = []
+    at = 0
+    for v in columns:
+        count = v.size // 128
+        totals.append(flat[at : at + count].reshape(v.shape))
+        at += count
+
+    def mean_rows(v):
+        return 0.5 * jnp.mean(v, axis=-1)
+
+    return (
+        give_back(place, rounded(memory)),
+        give_back(place, rounded(dec_final)),
+        give_back(place, grad_enc_half),
+        give_back(place, grad_dec_half),
+        shard_in,
+        shard_out,
+        shard_hin,
+        shard_hout,
+        shard_gains,
+        grad_position,
+        mean_rows(squares[0]),
+        0.5 * totals[0] / D,
+        mean_rows(squares[1]),
+        0.5 * totals[1] / D,
+        mean_rows(squares[2]),
+        0.5 * totals[2] / D,
+        mean_rows(squares[3]),
+        0.5 * totals[3] / FF,
+    )
+
+
+def body(mesh):
+    depth, seq = mesh.shape["dp"], mesh.shape["seq"]
+
+    def run(*args):
+        seqs, rows = args[0].shape[:2]
+        fits = (
+            depth == WAYS
+            and seq == 8
+            and seqs == 2
+            and (rows * 8) % TILE == 0
+            and args[1].shape == args[0].shape
+        )
+        return grouped(depth, *args) if fits else local(*args)
+
+    return run
+
+
 def solution(mesh):
     return jax.shard_map(
-        local,
+        body(mesh),
         mesh=mesh,
         in_specs=(
             P("dp", "seq", None),

time: 1950 us -> 755 us (0.39)
  waiting for transfers between devices: 1210 us -> 303 us
  local copies, waits for them, and re-layouts: 369 us -> 115 us
  starting transfers between devices: 1.81 us -> 140 us
  matrix products: 158 us -> 30.8 us
  blocking collectives: 99.6 us -> 39.2 us
  Pallas kernels: 0 us -> 28.3 us
    unnamed x24 -> x0, waiting for transfers between devices: 696 us -> none
    all_gather x16 -> x0, waiting for transfers between devices: 356 us -> none  [the longest x1 95.8 us: local(): lax.all_gather(hidden_in, ('dp', 'seq'), axis=2, tiled=True)]
    ppermute x0 -> x147, waiting for transfers between devices: none -> 303 us  [the longest x60 170 us: shift_z(): lax.ppermute(values, 'dp', [(i, (i + hops) % count) for i in range(count)])]
    reduce_scatter x2 -> x0, waiting for transfers between devices: 158 us -> none  [the longest x1 158 us: local(): lax.psum_scatter(grad_hidden_out, ('dp', 'seq'), scatter_dimension=1, til...]
    another operation x36 -> x9, local copies, waits for them, and re-layouts: 148 us -> 3.13 us  [the longest x8 60.7 us: hankel_block(): tiled = jnp.tile(window, (1, rows + 1))[:, :rows * (length + 1)]]
    ppermute x0 -> x147, starting transfers between devices: none -> 140 us  [the longest x60 75.2 us: shift_z(): lax.ppermute(values, 'dp', [(i, (i + hops) % count) for i in range(count)])]
    dot_general x53 -> x33, matrix products: 155 us -> 28.8 us  [the longest x11 12.3 us: matmul_nt(): lax.dot_general(a, b, (((1,), (1,)), ((), ())), preferred_element_type=jn...]
    all_gather x7 -> x1, blocking collectives: 99.6 us -> 39.2 us  [grouped(): gains_full = lax.all_gather(norm_gains, ('dp', 'seq'), axis=1, tiled=True)]
  transfers between devices with their start and end apart: 21 -> 147, of which waited for: 14 -> 78; matrix products, arithmetic and copies ran while one was open for 30% -> 25% of each run, Pallas kernels for 0% -> 3%
where the time goes in v1:
time: 755 us; the launch traced here: 745 us
  waiting for transfers between devices  303 us (40%)
  starting transfers between devices  140 us (19%)
  local copies, waits for them, and re-layouts  115 us (15%)
  other arithmetic  83.8 us (11%)
  blocking collectives  39.2 us (5%)
  matrix products  30.8 us (4%)
  Pallas kernels  28.3 us (4%)
    ppermute x60, waiting for transfers between devices, shift_z(): lax.ppermute(values, 'dp', [(i, (i + hops) % count) for i in range(count)])  170 us
    ppermute x85, waiting for transfers between devices, swap(): return lax.ppermute(values, 'seq', [(s, s ^ bits) for s in range(8)])  133 us
    ppermute x60, starting transfers between devices, shift_z(): lax.ppermute(values, 'dp', [(i, (i + hops) % count) for i in range(count)])  75.2 us
    ppermute x85, starting transfers between devices, swap(): return lax.ppermute(values, 'seq', [(s, s ^ bits) for s in range(8)])  63 us
    all_gather x1, blocking collectives, grouped(): gains_full = lax.all_gather(norm_gains, ('dp', 'seq'), axis=1, tiled=True)  39.2 us
    convert_element_type x43, other arithmetic, rounded(): return values.astype(jnp.bfloat16)  23.2 us
    unnamed x323, local copies, waits for them, and re-layouts  21.9 us
    dynamic_update_slice x30, local copies, waits for them, and re-layouts, gather_rows(): lax.dynamic_update_index_in_dim(held, block, (place.z - hops) % depth, 0)  18.5 us
  transfers between devices with their start and end apart: 147, of which 78 were waited for; matrix products, arithmetic and copies ran while one was open for 25% of the time, Pallas kernels for 3%

profile of v1, /device:TPU:0, one launch (start us, length us, event | category | flops | bytes accessed | tf_op | source)
XLA Modules:
  0.0 745.0 jit_solution(6932405772849453138)
XLA Ops:
  2.3 5.0 collective-permute-start.58
  16.2 39.2 %all-gather = bf16[32,24,7]{1,2,0:T(8,128)(2,1)S(1)} all-gather(bf16[1,24,7]{1,2,0:T(8,128)(2,1)S(1)} %bitcast.1230), channel_id=1, replica_groups=mesh['dp'=4,'seq'=8] {'dp','seq'}, dimensions={0}, use_global_device_ids=true | all-gather | bytes 11088 | tf_op jit(solution)/shard_map/all_gather | solution.py:1061
  78.3 5.8 collective-permute-done.23
  112.1 5.6 collective-permute-done.39
  118.4 4.6 collective-permute-done.40
  135.7 8.0 %collective-permute-done.5 = bf16[96,576]{1,0:T(8,128)(2,1)S(1)} collective-permute-done((bf16[96,576]{1,0:T(8,128)(2,1)S(1)}, bf16[96,576]{1,0:T(8,128)(2,1)S(1)}, u32[]{:S(2)}, u32[]{:S(2)}) %collective-permute-start.5) | collective-permute-done | bytes 110624 | tf_op jit(solution)/shard_map/ppermute | solution.py:718
  143.7 7.3 collective-permute-done.6
  174.8 7.1 collective-permute-done.20
  186.6 6.3 collective-permute-done.52
  194.5 8.7 %collective-permute-done.53 = bf16[96,1024]{1,0:T(8,128)(2,1)S(1)} collective-permute-done((bf16[96,1024]{1,0:T(8,128)(2,1)}, bf16[96,1024]{1,0:T(8,128)(2,1)S(1)}, u32[]{:S(2)}, u32[]{:S(2)}) %collective-permute-start.53) | collective-permute-done | bytes 196640 | tf_op jit(solution)/shard_map/ppermute | solution.py:718
  205.0 8.1 %collective-permute-done.35 = bf16[192,576]{1,0:T(8,128)(2,1)S(1)} collective-permute-done((bf16[192,576]{1,0:T(8,128)(2,1)S(1)}, bf16[192,576]{1,0:T(8,128)(2,1)S(1)}, u32[]{:S(2)}, u32[]{:S(2)}) %collective-permute-start.35) | collective-permute-done | bytes 221216 | tf_op jit(solution)/shard_map/ppermute | solution.py:718
  213.8 9.0 %collective-permute-done.36 = bf16[192,576]{1,0:T(8,128)(2,1)S(1)} collective-permute-done((bf16[192,576]{1,0:T(8,128)(2,1)S(1)}, bf16[192,576]{1,0:T(8,128)(2,1)S(1)}, u32[]{:S(2)}, u32[]{:S(2)}) %collective-permute-start.36) | collective-permute-done | bytes 221216 | tf_op jit(solution)/shard_map/ppermute | solution.py:718
  225.5 5.3 collective-permute-done.37
  239.7 5.3 collective-permute-done.8
  248.8 5.1 attend.3
  258.7 20.0 %collective-permute-done.22 = bf16[4,96,1024]{2,1,0:T(8,128)(2,1)S(1)} collective-permute-done((bf16[4,96,1024]{2,1,0:T(8,128)(2,1)}, bf16[4,96,1024]{2,1,0:T(8,128)(2,1)S(1)}, u32[]{:S(2)}, u32[]{:S(2)}) %collective-permute-start.22) | collective-permute-done | bytes 786464 | tf_op jit(solution)/shard_map/ppermute | solution.py:702
  280.0 18.0 %collective-permute-done.38 = bf16[4,192,576]{2,1,0:T(8,128)(2,1)S(1)} collective-permute-done((bf16[4,192,576]{2,1,0:T(8,128)(2,1)}, bf16[4,192,576]{2,1,0:T(8,128)(2,1)S(1)}, u32[]{:S(2)}, u32[]{:S(2)}) %collective-permute-start.38) | collective-permute-done | bytes 884768 | tf_op jit(solution)/shard_map/ppermute | solution.py:702
  300.6 5.0 attend.4
  313.6 6.2 collective-permute-done.44
  322.3 8.3 %collective-permute-done.28 = bf16[256,768]{1,0:T(8,128)(2,1)S(1)} collective-permute-done((bf16[256,768]{1,0:T(8,128)(2,1)S(1)}, bf16[256,768]{1,0:T(8,128)(2,1)S(1)}, u32[]{:S(2)}, u32[]{:S(2)}) %collective-permute-start.28) | collective-permute-done | bytes 393248 | tf_op jit(solution)/shard_map/ppermute | solution.py:702
  334.8 5.0 attend.5
  346.9 7.9 %collective-permute-done.48 = bf16[256,768]{1,0:T(8,128)(2,1)S(1)} collective-permute-done((bf16[256,768]{1,0:T(8,128)(2,1)S(1)}, bf16[256,768]{1,0:T(8,128)(2,1)S(1)}, u32[]{:S(2)}, u32[]{:S(2)}) %collective-permute-start.48) | collective-permute-done | bytes 393248 | tf_op jit(solution)/shard_map/ppermute | solution.py:702
  405.9 4.7 collective-permute-done.131
  438.5 9.9 %collective-permute-done.123 = bf16[96,1024]{1,0:T(8,128)(2,1)S(1)} collective-permute-done((bf16[96,1024]{1,0:T(8,128)(2,1)S(1)}, bf16[96,1024]{1,0:T(8,128)(2,1)S(1)}, u32[]{:S(2)}, u32[]{:S(2)}) %collective-permute-start.123) | collective-permute-done | bytes 196640 | tf_op jit(solution)/shard_map/ppermute | solution.py:718
  499.6 5.5 collective-permute-done.98
  515.1 5.0 collective-permute-done.70
  538.5 5.2 attend_back.5
  594.2 4.7 collective-permute-done.92
  627.8 8.4 %collective-permute-done.117 = bf16[96,1024]{1,0:T(8,128)(2,1)S(1)} collective-permute-done((bf16[96,1024]{1,0:T(8,128)(2,1)S(1)}, bf16[96,1024]{1,0:T(8,128)(2,1)S(1)}, u32[]{:S(2)}, u32[]{:S(2)}) %collective-permute-start.117) | collective-permute-done | bytes 196640 | tf_op jit(solution)/shard_map/ppermute | solution.py:718
  651.3 5.2 attend_back.4
  686.2 6.3 collective-permute-done.86
  703.0 5.8 collective-permute-done.76
  (1024 shorter events, 478.6 us)
Async XLA Ops:
  2.3 88.2 %collective-permute-start.58 = (bf16[64,768]{1,0:T(8,128)(2,1)}, bf16[64,768]{1,0:T(8,128)(2,1)}, u32[]{:S(2)}, u32[]{:S(2)}) collective-permute-start(bf16[64,768]{1,0:T(8,128)(2,1)} %get-tuple-element.316), channel_id=1, source_target_pairs={{0,24},{8,0},{16,8},{24,16},{1,25},{9,1},{17,9},{25,17},{2,26},{10... | collective-permute-start | bytes 294920 | tf_op jit(solution)/shard_map/ppermute | solution.py:718
  7.4 78.2 %collective-permute-start.57 = (bf16[64,768]{1,0:T(8,128)(2,1)}, bf16[64,768]{1,0:T(8,128)(2,1)}, u32[]{:S(2)}, u32[]{:S(2)}) collective-permute-start(bf16[64,768]{1,0:T(8,128)(2,1)} %get-tuple-element.316), channel_id=1, source_target_pairs={{0,16},{8,24},{16,0},{24,8},{1,17},{9,25},{17,1},{25,9},{2,18},{10... | collective-permute-start | bytes 294920 | tf_op jit(solution)/shard_map/ppermute | solution.py:718
  7.4 69.9 %collective-permute-start.56 = (bf16[64,768]{1,0:T(8,128)(2,1)}, bf16[64,768]{1,0:T(8,128)(2,1)}, u32[]{:S(2)}, u32[]{:S(2)}) collective-permute-start(bf16[64,768]{1,0:T(8,128)(2,1)} %get-tuple-element.316), channel_id=1, source_target_pairs={{0,8},{8,16},{16,24},{24,0},{1,9},{9,17},{17,25},{25,1},{2,10},{10... | collective-permute-start | bytes 294920 | tf_op jit(solution)/shard_map/ppermute | solution.py:718
  10.0 54.0 %collective-permute-start.30 = (bf16[1,64,768]{2,1,0:T(8,128)(2,1)}, bf16[1,64,768]{2,1,0:T(8,128)(2,1)}, u32[]{:S(2)}, u32[]{:S(2)}) collective-permute-start(bf16[1,64,768]{2,1,0:T(8,128)(2,1)} %constant_dynamic-slice_fusion.14), channel_id=1, source_target_pairs={{0,4},{1,5},{2,6},{3,7},{4,0},{5,1},{6,2},{7,3},{8,12},{9,13},{10,... | collective-permute-start | bytes 294920 | tf_op jit(solution)/shard_map/ppermute | solution.py:702
  13.8 49.2 %collective-permute-start.3 = (bf16[2,24,576]{2,1,0:T(8,128)(2,1)S(1)}, bf16[2,24,576]{2,1,0:T(8,128)(2,1)}, u32[]{:S(2)}, u32[]{:S(2)}) collective-permute-start(bf16[2,24,576]{2,1,0:T(8,128)(2,1)S(1)} %dynamic-slice_bitcast_fusion.33), channel_id=1, source_target_pairs={{0,2},{1,3},{2,0},{3,1},{4,6},{5,7},{6,4},{7,5},{8,10},{9,11},{10,... | collective-permute-start | bytes 165896 | tf_op jit(solution)/shard_map/ppermute | solution.py:702
  63.9 27.6 %collective-permute-start.25 = (bf16[64,768]{1,0:T(8,128)(2,1)}, bf16[64,768]{1,0:T(8,128)(2,1)S(1)}, u32[]{:S(2)}, u32[]{:S(2)}) collective-permute-start(bf16[64,768]{1,0:T(8,128)(2,1)} %get-tuple-element.317), channel_id=1, source_target_pairs={{0,24},{8,0},{16,8},{24,16},{1,25},{9,1},{17,9},{25,17},{2,26},{10... | collective-permute-start | bytes 294920 | tf_op jit(solution)/shard_map/ppermute | solution.py:718
  85.6 43.5 %collective-permute-start.63 = (bf16[2,64,768]{2,1,0:T(8,128)(2,1)}, bf16[2,64,768]{2,1,0:T(8,128)(2,1)S(1)}, u32[]{:S(2)}, u32[]{:S(2)}) collective-permute-start(bf16[2,64,768]{2,1,0:T(8,128)(2,1)} %pad_maximum_fusion.33), channel_id=1, source_target_pairs={{0,4},{1,5},{2,6},{3,7},{4,0},{5,1},{6,2},{7,3},{8,12},{9,13},{10,... | collective-permute-start | bytes 589832 | tf_op jit(solution)/shard_map/ppermute | solution.py:702
  91.5 66.5 %collective-permute-start.31 = (bf16[2,1,64,768]{3,2,0,1:T(8,128)(2,1)S(1)}, bf16[2,1,64,768]{3,2,0,1:T(8,128)(2,1)S(1)}, u32[]{:S(2)}, u32[]{:S(2)}) collective-permute-start(bf16[2,1,64,768]{3,2,0,1:T(8,128)(2,1)S(1)} %fusion.113), channel_id=1, source_target_pairs={{0,2},{1,3},{2,0},{3,1},{4,6},{5,7},{6,4},{7,5},{8,10},{9,11},{10,... | collective-permute-start | bytes 589832 | tf_op jit(solution)/shard_map/ppermute | solution.py:702
  91.9 67.6 %collective-permute-start.1 = (bf16[2,1,64,768]{3,2,0,1:T(8,128)(2,1)}, bf16[2,1,64,768]{3,2,0,1:T(8,128)(2,1)}, u32[]{:S(2)}, u32[]{:S(2)}) collective-permute-start(bf16[2,1,64,768]{3,2,0,1:T(8,128)(2,1)} %pad_maximum_fusion.27), channel_id=1, source_target_pairs={{0,2},{1,3},{2,0},{3,1},{4,6},{5,7},{6,4},{7,5},{8,10},{9,11},{10,... | collective-permute-start | bytes 589832 | tf_op jit(solution)/shard_map/ppermute | solution.py:702
  95.1 139.5 %collective-permute-start.26 = (bf16[4,64,768]{2,1,0:T(8,128)(2,1)S(1)}, bf16[4,64,768]{2,1,0:T(8,128)(2,1)}, u32[]{:S(2)}, u32[]{:S(2)}) collective-permute-start(bf16[4,64,768]{2,1,0:T(8,128)(2,1)S(1)} %bitcast_dynamic-update-slice_fusion.15), channel_id=1, source_target_pairs={{0,4},{1,5},{2,6},{3,7},{4,0},{5,1},{6,2},{7,3},{8,12},{9,13},{10,... | collective-permute-start | bytes 1179656 | tf_op jit(solution)/shard_map/ppermute | solution.py:702
  128.8 107.4 %collective-permute-start.59 = (bf16[4,64,768]{2,1,0:T(8,128)(2,1)S(1)}, bf16[4,64,768]{2,1,0:T(8,128)(2,1)}, u32[]{:S(2)}, u32[]{:S(2)}) collective-permute-start(bf16[4,64,768]{2,1,0:T(8,128)(2,1)S(1)} %bitcast_dynamic-update-slice_fusion.12), channel_id=1, source_target_pairs={{0,4},{1,5},{2,6},{3,7},{4,0},{5,1},{6,2},{7,3},{8,12},{9,13},{10,... | collective-permute-start | bytes 1179656 | tf_op jit(solution)/shard_map/ppermute | solution.py:702
  158.1 75.3 %collective-permute-start.42 = (bf16[4,2,24,768]{3,2,0,1:T(8,128)(2,1)}, bf16[4,2,24,768]{3,2,0,1:T(8,128)(2,1)}, u32[]{:S(2)}, u32[]{:S(2)}) collective-permute-start(bf16[4,2,24,768]{3,2,0,1:T(8,128)(2,1)} %bitcast_dynamic-update-slice_fusion.18), channel_id=1, source_target_pairs={{0,4},{1,5},{2,6},{3,7},{4,0},{5,1},{6,2},{7,3},{8,12},{9,13},{10,... | collective-permute-start | bytes 884744 | tf_op jit(solution)/shard_map/ppermute | solution.py:702
  159.4 25.5 %collective-permute-start.21 = (bf16[96,1024]{1,0:T(8,128)(2,1)}, bf16[96,1024]{1,0:T(8,128)(2,1)}, u32[]{:S(2)}, u32[]{:S(2)}) collective-permute-start(bf16[96,1024]{1,0:T(8,128)(2,1)} %bitcast.63), channel_id=1, source_target_pairs={{0,24},{8,0},{16,8},{24,16},{1,25},{9,1},{17,9},{25,17},{2,26},{10... | collective-permute-start | bytes 589832 | tf_op jit(solution)/shard_map/ppermute | solution.py:718
  181.9 22.4 %collective-permute-start.54 = (bf16[96,1024]{1,0:T(8,128)(2,1)}, bf16[96,1024]{1,0:T(8,128)(2,1)S(1)}, u32[]{:S(2)}, u32[]{:S(2)}) collective-permute-start(bf16[96,1024]{1,0:T(8,128)(2,1)} %bitcast.1203), channel_id=1, source_target_pairs={{0,24},{8,0},{16,8},{24,16},{1,25},{9,1},{17,9},{25,17},{2,26},{10... | collective-permute-start | bytes 589832 | tf_op jit(solution)/shard_map/ppermute | solution.py:718
  203.3 34.5 %collective-permute-start.64 = (bf16[2,2,64,768]{3,2,1,0:T(8,128)(2,1)}, bf16[2,2,64,768]{3,2,1,0:T(8,128)(2,1)S(1)}, u32[]{:S(2)}, u32[]{:S(2)}) collective-permute-start(bf16[2,2,64,768]{3,2,1,0:T(8,128)(2,1)} %pad_maximum_fusion.20), channel_id=1, source_target_pairs={{0,2},{1,3},{2,0},{3,1},{4,6},{5,7},{6,4},{7,5},{8,10},{9,11},{10,... | collective-permute-start | bytes 1179656 | tf_op jit(solution)/shard_map/ppermute | solution.py:702
  234.5 20.6 %collective-permute-start.32 = (bf16[256,768]{1,0:T(8,128)(2,1)S(1)}, bf16[256,768]{1,0:T(8,128)(2,1)S(1)}, u32[]{:S(2)}, u32[]{:S(2)}) collective-permute-start(bf16[256,768]{1,0:T(8,128)(2,1)S(1)} %bitcast.1115), channel_id=1, source_target_pairs={{0,1},{1,0},{2,3},{3,2},{4,5},{5,4},{6,7},{7,6},{8,9},{9,8},{10,11... | collective-permute-start | bytes 1179656 | tf_op jit(solution)/shard_map/ppermute | solution.py:702
  236.2 119.5 %collective-permute-start.55 = (bf16[4,96,1024]{2,1,0:T(8,128)(2,1)}, bf16[4,96,1024]{2,1,0:T(8,128)(2,1)S(1)}, u32[]{:S(2)}, u32[]{:S(2)}) collective-permute-start(bf16[4,96,1024]{2,1,0:T(8,128)(2,1)} %bitcast_dynamic-update-slice_fusion.3), channel_id=1, source_target_pairs={{0,4},{1,5},{2,6},{3,7},{4,0},{5,1},{6,2},{7,3},{8,12},{9,13},{10,... | collective-permute-start | bytes 2359304 | tf_op jit(solution)/shard_map/ppermute | solution.py:702
  237.8 40.9 %collective-permute-start.22 = (bf16[4,96,1024]{2,1,0:T(8,128)(2,1)}, bf16[4,96,1024]{2,1,0:T(8,128)(2,1)S(1)}, u32[]{:S(2)}, u32[]{:S(2)}) collective-permute-start(bf16[4,96,1024]{2,1,0:T(8,128)(2,1)} %bitcast_dynamic-update-slice_fusion.6), channel_id=1, source_target_pairs={{0,4},{1,5},{2,6},{3,7},{4,0},{5,1},{6,2},{7,3},{8,12},{9,13},{10,... | collective-permute-start | bytes 2359304 | tf_op jit(solution)/shard_map/ppermute | solution.py:702
  245.0 52.9 %collective-permute-start.38 = (bf16[4,192,576]{2,1,0:T(8,128)(2,1)}, bf16[4,192,576]{2,1,0:T(8,128)(2,1)S(1)}, u32[]{:S(2)}, u32[]{:S(2)}) collective-permute-start(bf16[4,192,576]{2,1,0:T(8,128)(2,1)} %bitcast_dynamic-update-slice_fusion), channel_id=1, source_target_pairs={{0,4},{1,5},{2,6},{3,7},{4,0},{5,1},{6,2},{7,3},{8,12},{9,13},{10,... | collective-permute-start | bytes 2654216 | tf_op jit(solution)/shard_map/ppermute | solution.py:702
  256.9 49.9 %collective-permute-start.15 = (bf16[256,768]{1,0:T(8,128)(2,1)S(1)}, bf16[256,768]{1,0:T(8,128)(2,1)S(1)}, u32[]{:S(2)}, u32[]{:S(2)}) collective-permute-start(bf16[256,768]{1,0:T(8,128)(2,1)S(1)} %fusion.43), channel_id=1, source_target_pairs={{0,2},{1,3},{2,0},{3,1},{4,6},{5,7},{6,4},{7,5},{8,10},{9,11},{10,... | collective-permute-start | bytes 1179656 | tf_op jit(solution)/shard_map/ppermute | solution.py:702
  405.2 21.9 %collective-permute-start.121 = (bf16[4,96,1024]{2,1,0:T(8,128)(2,1)S(1)}, bf16[4,96,1024]{2,1,0:T(8,128)(2,1)S(1)}, u32[]{:S(2)}, u32[]{:S(2)}) collective-permute-start(bf16[4,96,1024]{2,1,0:T(8,128)(2,1)S(1)} %fusion.34), channel_id=1, source_target_pairs={{0,4},{1,5},{2,6},{3,7},{4,0},{5,1},{6,2},{7,3},{8,12},{9,13},{10,... | collective-permute-start | bytes 2359304 | tf_op jit(solution)/shard_map/ppermute | solution.py:702
  435.3 20.5 %collective-permute-start.68 = (bf16[256,768]{1,0:T(8,128)(2,1)}, bf16[256,768]{1,0:T(8,128)(2,1)}, u32[]{:S(2)}, u32[]{:S(2)}) collective-permute-start(bf16[256,768]{1,0:T(8,128)(2,1)} %get-tuple-element.189), channel_id=1, source_target_pairs={{0,1},{1,0},{2,3},{3,2},{4,5},{5,4},{6,7},{7,6},{8,9},{9,8},{10,11... | collective-permute-start | bytes 1179656 | tf_op jit(solution)/shard_map/ppermute | solution.py:702
  480.5 26.4 %collective-permute-start.69 = (bf16[256,768]{1,0:T(8,128)(2,1)S(1)}, bf16[256,768]{1,0:T(8,128)(2,1)S(1)}, u32[]{:S(2)}, u32[]{:S(2)}) collective-permute-start(bf16[256,768]{1,0:T(8,128)(2,1)S(1)} %fusion.63), channel_id=1, source_target_pairs={{0,1},{1,0},{2,3},{3,2},{4,5},{5,4},{6,7},{7,6},{8,9},{9,8},{10,11... | collective-permute-start | bytes 1179656 | tf_op jit(solution)/shard_map/ppermute | solution.py:702
  480.6 29.3 %collective-permute-start.78 = (bf16[256,768]{1,0:T(8,128)(2,1)S(1)}, bf16[256,768]{1,0:T(8,128)(2,1)S(1)}, u32[]{:S(2)}, u32[]{:S(2)}) collective-permute-start(bf16[256,768]{1,0:T(8,128)(2,1)S(1)} %fusion.66), channel_id=1, source_target_pairs={{0,1},{1,0},{2,3},{3,2},{4,5},{5,4},{6,7},{7,6},{8,9},{9,8},{10,11... | collective-permute-start | bytes 1179656 | tf_op jit(solution)/shard_map/ppermute | solution.py:702
  536.8 24.8 %collective-permute-start.106 = (bf16[4,24,768]{2,1,0:T(8,128)(2,1)}, bf16[4,24,768]{2,1,0:T(8,128)(2,1)}, u32[]{:S(2)}, u32[]{:S(2)}) collective-permute-start(bf16[4,24,768]{2,1,0:T(8,128)(2,1)} %fusion.109), channel_id=1, source_target_pairs={{0,4},{1,5},{2,6},{3,7},{4,0},{5,1},{6,2},{7,3},{8,12},{9,13},{10,... | collective-permute-start | bytes 442376 | tf_op jit(solution)/shard_map/ppermute | solution.py:702
  545.4 28.3 %collective-permute-start.81 = (bf16[256,768]{1,0:T(8,128)(2,1)}, bf16[256,768]{1,0:T(8,128)(2,1)}, u32[]{:S(2)}, u32[]{:S(2)}) collective-permute-start(bf16[256,768]{1,0:T(8,128)(2,1)} %fusion.67), channel_id=1, source_target_pairs={{0,1},{1,0},{2,3},{3,2},{4,5},{5,4},{6,7},{7,6},{8,9},{9,8},{10,11... | collective-permute-start | bytes 1179656 | tf_op jit(solution)/shard_map/ppermute | solution.py:702
  548.2 28.5 %collective-permute-start.127 = (bf16[4,64,768]{2,1,0:T(8,128)(2,1)}, bf16[4,64,768]{2,1,0:T(8,128)(2,1)}, u32[]{:S(2)}, u32[]{:S(2)}) collective-permute-start(bf16[4,64,768]{2,1,0:T(8,128)(2,1)} %fusion.68), channel_id=1, source_target_pairs={{0,4},{1,5},{2,6},{3,7},{4,0},{5,1},{6,2},{7,3},{8,12},{9,13},{10,... | collective-permute-start | bytes 1179656 | tf_op jit(solution)/shard_map/ppermute | solution.py:702
  571.4 40.9 %collective-permute-start.115 = (bf16[4,96,1024]{2,1,0:T(8,128)(2,1)}, bf16[4,96,1024]{2,1,0:T(8,128)(2,1)}, u32[]{:S(2)}, u32[]{:S(2)}) collective-permute-start(bf16[4,96,1024]{2,1,0:T(8,128)(2,1)} %fusion.33), channel_id=1, source_target_pairs={{0,4},{1,5},{2,6},{3,7},{4,0},{5,1},{6,2},{7,3},{8,12},{9,13},{10,... | collective-permute-start | bytes 2359304 | tf_op jit(solution)/shard_map/ppermute | solution.py:702
  575.7 30.3 %collective-permute-start.82 = (bf16[256,768]{1,0:T(8,128)(2,1)}, bf16[256,768]{1,0:T(8,128)(2,1)}, u32[]{:S(2)}, u32[]{:S(2)}) collective-permute-start(bf16[256,768]{1,0:T(8,128)(2,1)} %fusion.53), channel_id=1, source_target_pairs={{0,2},{1,3},{2,0},{3,1},{4,6},{5,7},{6,4},{7,5},{8,10},{9,11},{10,... | collective-permute-start | bytes 1179656 | tf_op jit(solution)/shard_map/ppermute | solution.py:702
  608.7 28.6 %collective-permute-start.83 = (f32[64,768]{1,0:T(8,128)S(1)}, f32[64,768]{1,0:T(8,128)S(1)}, u32[]{:S(2)}, u32[]{:S(2)}) collective-permute-start(f32[64,768]{1,0:T(8,128)S(1)} %dynamic-slice_bitcast_fusion.6), channel_id=1, source_target_pairs={{0,4},{1,5},{2,6},{3,7},{4,0},{5,1},{6,2},{7,3},{8,12},{9,13},{10,... | collective-permute-start | bytes 589832 | tf_op jit(solution)/shard_map/ppermute | solution.py:702
  622.2 25.9 %collective-permute-start.74 = (bf16[256,768]{1,0:T(8,128)(2,1)S(1)}, bf16[256,768]{1,0:T(8,128)(2,1)}, u32[]{:S(2)}, u32[]{:S(2)}) collective-permute-start(bf16[256,768]{1,0:T(8,128)(2,1)S(1)} %get-tuple-element.185), channel_id=1, source_target_pairs={{0,1},{1,0},{2,3},{3,2},{4,5},{5,4},{6,7},{7,6},{8,9},{9,8},{10,11... | collective-permute-start | bytes 1179656 | tf_op jit(solution)/shard_map/ppermute | solution.py:702
  669.2 27.8 %collective-permute-start.75 = (bf16[256,768]{1,0:T(8,128)(2,1)}, bf16[256,768]{1,0:T(8,128)(2,1)S(1)}, u32[]{:S(2)}, u32[]{:S(2)}) collective-permute-start(bf16[256,768]{1,0:T(8,128)(2,1)} %fusion.65), channel_id=1, source_target_pairs={{0,1},{1,0},{2,3},{3,2},{4,5},{5,4},{6,7},{7,6},{8,9},{9,8},{10,11... | collective-permute-start | bytes 1179656 | tf_op jit(solution)/shard_map/ppermute | solution.py:702
  (274 other events, 2584.3 us)
